TPU v7x, 128 devices: a whole 4x4x4 slice. The times are simulated.
128 devices in a mesh: sess: 16 (over y_lo, z, core), tp: 8 (over y_hi, x).
Axes of the slice: x: 4, y: 4 (y_hi: 2, y_lo: 2; y = y_hi * 2 + y_lo), z: 4, core: 2. Of those that a mesh axis runs over, the one named last changes fastest.
Arguments:
- x_resid: bfloat16 [256, 8192], P(None, 'sess'), may hold values from -18 to 18
- qkv_new: bfloat16 [256, 8, 1280], P('sess', 'tp'), may hold values from -60 to 60
- kv_cache: bfloat16 [256, 2, 8, 1024, 128], P('sess', None, 'tp'), may hold values from -8 to 8
- cache_lens: int32 [256], P('sess'), may hold values from 1 to 1024, as said below
- wo_temporal: bfloat16 [8192, 8192], P('tp', 'sess'), may hold values from -0.0625 to 0.0625
- norm_gain: float32 [8192], P('sess'), may hold values from 0.1 to 1.9
- w_in: bfloat16 [8, 8192, 1024], P('tp', 'sess'), may hold values from -0.0625 to 0.0625
- embed_rows: bfloat16 [8, 2048, 1024], P('tp', 'sess'), may hold values from -6 to 6
- token_ids: int32 [256, 8], P(None, 'tp'), may hold values from 0 to 2047
- depth_gain: float32 [8, 1024], P('tp'), may hold values from 0.1 to 1.9
- depth_qkv: bfloat16 [8, 1024, 3072], P('tp'), may hold values from -6 to 6
- depth_out: bfloat16 [8, 1024, 1024], P('tp'), may hold values from -0.1875 to 0.1875
Outputs:
- depth_hidden: bfloat16 [256, 8, 1024], P('sess', 'tp')
Inputs may be any that keep to these rules, and one draw needn't show every extreme that they name: `cache_lens`: some session has exactly 1024 live frames.
All inputs are finite; a program needn't handle non-finite values.
Results may differ from a plain program's by a relative error of at most 0.009.
Values may be sent and summed in bfloat16 or wider, within the bound.
A program may use at most 64 MiB of HBM per device.

v0:
```python
import jax
import jax.numpy as jnp
from jax import lax
from jax.sharding import PartitionSpec as P

D = 8192
DHEADS = 16


EPS = 1e-05


def temporal_attention(qkv_new, kv_cache, cache_lens):
    sess_rows = kv_cache.shape[0]
    kv_local = kv_cache.shape[2]
    cache_frames = kv_cache.shape[3]
    head_size = kv_cache.shape[4]
    group = qkv_new.shape[2] // head_size - 2
    queries = qkv_new[:, :, : group * head_size].reshape(sess_rows, kv_local, group, head_size)
    new_key = qkv_new[:, :, group * head_size : (group + 1) * head_size]
    new_value = qkv_new[:, :, (group + 1) * head_size :]
    score_scale = head_size ** (-0.5)
    old_scores = (
        jnp.einsum("skgd,skld->skgl", queries, kv_cache[:, 0], preferred_element_type=jnp.float32)
        * score_scale
    )
    new_scores = (
        jnp.einsum("skgd,skd->skg", queries, new_key, preferred_element_type=jnp.float32)
        * score_scale
    )
    frames = lax.broadcasted_iota(jnp.int32, (1, 1, 1, cache_frames), 3)
    visible = frames < cache_lens[:, None, None, None]
    peak_score = jnp.maximum(jnp.max(jnp.where(visible, old_scores, -1e30), axis=-1), new_scores)
    old_exp = jnp.where(visible, jnp.exp(old_scores - peak_score[..., None]), 0.0)
    new_exp = jnp.exp(new_scores - peak_score)
    summed_exp = jnp.sum(old_exp, axis=-1) + new_exp
    old_weights = (old_exp / summed_exp[..., None]).astype(jnp.bfloat16)
    new_weights = (new_exp / summed_exp).astype(jnp.bfloat16)
    context = jnp.einsum(
        "skgl,skld->skgd", old_weights, kv_cache[:, 1], preferred_element_type=jnp.float32
    )
    context = (
        context
        + new_weights.astype(jnp.float32)[..., None] * new_value.astype(jnp.float32)[:, :, None, :]
    )
    return context.astype(jnp.bfloat16).reshape(sess_rows, kv_local * group * head_size)


def normalize_rows(hidden, squares, norm_gain):
    scaled = hidden * lax.rsqrt(squares / D + EPS)[:, None] * norm_gain[None, :]
    return scaled.astype(jnp.bfloat16)


def shards(
    x_resid,
    qkv_new,
    kv_cache,
    cache_lens,
    wo_temporal,
    norm_gain,
    w_in,
    embed_rows,
    token_ids,
    depth_gain,
    depth_qkv,
    depth_out,
):
    sess_rows = kv_cache.shape[0]
    attn_rows = temporal_attention(qkv_new, kv_cache, cache_lens)
    partial_out = jnp.dot(
        lax.all_gather(attn_rows, "sess", axis=0, tiled=True),
        wo_temporal,
        preferred_element_type=jnp.float32,
    )
    summed = lax.psum(partial_out, "tp")
    hidden = x_resid.astype(jnp.float32) + summed
    squares = lax.psum(jnp.sum(hidden * hidden, axis=1), "sess")
    normed = normalize_rows(hidden, squares, norm_gain)
    cb_local = w_in.shape[0]
    depth_width = w_in.shape[2]
    vocab_rows = embed_rows.shape[1]
    vocab_start = lax.axis_index("sess") * vocab_rows
    vocab_iota = lax.broadcasted_iota(jnp.int32, (1, 1, vocab_rows), 2)
    projected = jnp.einsum("rd,cde->rce", normed, w_in, preferred_element_type=jnp.float32)
    one_hot = (token_ids[:, :, None] - vocab_start == vocab_iota).astype(jnp.bfloat16)
    looked = jnp.einsum("rcv,cve->rce", one_hot, embed_rows, preferred_element_type=jnp.float32)
    depth_flat = lax.psum_scatter(
        (projected + looked).reshape(sess_rows * lax.axis_size("sess"), cb_local * depth_width),
        "sess",
        scatter_dimension=0,
        tiled=True,
    )
    depth_in = depth_flat.reshape(sess_rows, cb_local, depth_width)
    mean_sq = jnp.mean(depth_in * depth_in, axis=-1)
    depth_normed = (depth_in * lax.rsqrt(mean_sq + EPS)[..., None] * depth_gain[None]).astype(
        jnp.bfloat16
    )
    depth_proj = jnp.einsum(
        "sce,cef->scf", depth_normed, depth_qkv, preferred_element_type=jnp.float32
    ).astype(jnp.bfloat16)
    head_size = depth_width // DHEADS
    queries = depth_proj[..., :depth_width].reshape(sess_rows, cb_local, DHEADS, head_size)
    key_values = depth_proj[..., depth_width:]
    owned = lax.axis_index("tp") * cb_local + lax.broadcasted_iota(jnp.int32, (cb_local,), 0)
    score_scale = head_size ** (-0.5)
    start_peak = jnp.full((sess_rows, cb_local, DHEADS), -1e30, jnp.float32)
    block_in = lax.all_gather(key_values, "tp", axis=1, tiled=True)
    positions = block_in.shape[1]
    block_keys = block_in[..., :depth_width].reshape(sess_rows, positions, DHEADS, head_size)
    block_values = block_in[..., depth_width:].reshape(sess_rows, positions, DHEADS, head_size)
    scores = (
        jnp.einsum("schd,snhd->schn", queries, block_keys, preferred_element_type=jnp.float32)
        * score_scale
    )
    key_pos = lax.broadcasted_iota(jnp.int32, (positions,), 0)
    visible = key_pos[None, None, None, :] <= owned[None, :, None, None]
    peak_next = jnp.maximum(start_peak, jnp.max(jnp.where(visible, scores, -1e30), axis=-1))
    expo = jnp.where(visible, jnp.exp(scores - peak_next[..., None]), 0.0)
    summed_next = jnp.sum(expo, axis=-1)
    accum_next = jnp.einsum("schn,snhd->schd", expo, block_values.astype(jnp.float32))
    depth_ctx = (
        (accum_next / summed_next[..., None])
        .reshape(sess_rows, cb_local, depth_width)
        .astype(jnp.bfloat16)
    )
    projected = jnp.einsum("sce,cef->scf", depth_ctx, depth_out, preferred_element_type=jnp.float32)
    return (depth_in + projected).astype(jnp.bfloat16)


def solution(mesh):
    in_specs = (
        P(None, "sess"),
        P("sess", "tp", None),
        P("sess", None, "tp", None, None),
        P("sess"),
        P("tp", "sess"),
        P("sess"),
        P("tp", "sess", None),
        P("tp", "sess", None),
        P(None, "tp"),
        P("tp", None),
        P("tp", None, None),
        P("tp", None, None),
    )
    out_specs = P("sess", "tp", None)
    return jax.shard_map(shards, mesh=mesh, in_specs=in_specs, out_specs=out_specs, check_vma=False)
```

profile of v0, /device:TPU:0, one launch (start us, length us, event | category | flops | bytes accessed | tf_op | source)
XLA Modules:
  0.0 264.0 jit_solution(9343530428508861457)
XLA Ops:
  6.5 0.0 copy-start
  6.5 0.0 all-reduce.2.cloned.1.call-start
  6.5 0.9 slice_bitcast_fusion
  7.4 0.7 bitcast_convert_fusion
  8.2 0.7 iota_compare_fusion.1
  8.9 0.1 fusion.56
  9.0 0.0 copy-start.3
  9.0 3.6 %select_reduce_fusion = (f32[16,8]{1,0:T(8,128)S(1)}, f32[16,8,1024]{2,1,0:T(8,128)S(1)}) fusion(pred[16,1024]{1,0:T(8,128)(4,1)S(1)} %iota_compare_fusion.1, bf16[16,8,128]{2,1,0:T(8,128)(2,1)S(1)} %bitcast.122, bf16[16,2,1,1024,128]{4,3,2,1,0:T(8,128)(2,1)} %param.14), kind=kOutput, calls=%fused_computation.27 | convolution fusion | flops 33947520 | bytes 4768256 | tf_op jit(solution)/shard_map/skgd,skld->skgl/dot_general | solution.py:24
  12.6 0.0 copy-start.7
  12.6 0.0 copy-start.6
  12.6 0.3 fusion.41
  12.9 3.0 %fusion.33 = bf16[16,8,128]{2,1,0:T(8,128)(2,1)S(1)} fusion(bf16[16,2,1,1024,128]{4,3,2,1,0:T(8,128)(2,1)} %param.14, f32[16,8,1024]{2,1,0:T(8,128)S(1)} %get-tuple-element.12, f32[16,8]{1,0:T(8,128)S(1)} %get-tuple-element.10, f32[16,8]{1,0:T(8,128)S(1)} %multiply_maximum_fusion, pred[16,1024]{1,0:T(8,128)(4,1)S(1)} %iota_compare_fusion.1, ...), kind=kOutput, calls=%fused_computation.21 | convolution fusion | flops 34127872 | bytes 4777472 | tf_op jit(solution)/shard_map/skgl,skld->skgd/dot_general | solution.py:39
  16.0 22.5 %all_gather.6 = bf16[256,1024]{1,0:T(8,128)(2,1)S(1)} all-gather(bf16[16,1024]{1,0:T(8,128)(2,1)S(1)} %bitcast.123), channel_id=1, replica_groups=mesh['sess'=16,'tp'=8] {'sess'}, dimensions={0}, use_global_device_ids=true | all-gather | bytes 557056 | tf_op jit(solution)/shard_map/all_gather | solution.py:71
  38.5 0.0 copy-done.3
  38.5 1.2 fusion.62
  39.7 0.0 all-reduce.2.cloned.1.call-update
  39.7 0.0 reduce-scatter.2.cloned.1.call-start
  39.8 0.0 copy-done.7
  39.8 84.0 %all-reduce.2.cloned.1.call-done = f32[256,512]{1,0:T(8,128)} async-done(((f32[256,512]{1,0:T(8,128)}), f32[256,512]{1,0:T(8,128)}) %all-reduce.2.cloned.1.call-update) | async-done | bytes 524304 | tf_op jit(solution)/shard_map/psum | solution.py:75
  123.8 0.0 copy-done.2
  123.8 1.2 multiply_reduce_fusion
  125.0 27.1 %psum.15 = f32[256]{0:T(256)S(1)} all-reduce(f32[256]{0:T(256)S(1)} %multiply_reduce_fusion), channel_id=1, replica_groups=mesh['sess'=16,'tp'=8] {'sess'}, use_global_device_ids=true, to_apply=%region_4.5 | all-reduce | flops 256 | bytes 2048 | tf_op jit(solution)/shard_map/psum | solution.py:77
  152.2 0.0 copy-done.1
  152.2 0.0 copy-done.6
  152.2 1.5 convolution_bitcast_fusion.1
  153.7 2.3 fusion.17
  156.0 0.0 reduce-scatter.2.cloned.1.call-update
  156.0 57.4 %reduce-scatter.2.cloned.1.call-done = f32[16,1024]{1,0:T(8,128)} async-done(((f32[256,1024]{1,0:T(8,128)}), f32[16,1024]{1,0:T(8,128)}) %reduce-scatter.2.cloned.1.call-update) | async-done | bytes 65552 | tf_op jit(solution)/shard_map/reduce_scatter | solution.py:87
  213.4 1.0 multiply_reduce_fusion.1
  214.3 0.0 copy-done.5
  214.3 0.0 copy-start.4
  214.4 3.8 %fusion.11 = bf16[16,1,3072]{2,0,1:T(8,128)(2,1)S(1)} fusion(bf16[1,1024,3072]{2,1,0:T(8,128)(2,1)} %param.22, f32[16,1024]{1,0:T(8,128)} %reduce-scatter.2.cloned.1.call-done, f32[1024]{0:T(1024)S(1)} %bitcast.129, f32[16]{0:T(128)S(1)} %add_rsqrt_fusion.1), kind=kOutput, calls=%fused_computation.9 | convolution fusion | flops 100761600 | bytes 6459456 | tf_op jit(solution)/shard_map/sce,cef->scf/dot_general | solution.py:98
  218.2 35.2 %all_gather.7 = bf16[16,8,2048]{2,0,1:T(8,128)(2,1)S(1)} all-gather(bf16[16,1,2048]{2,0,1:T(8,128)(2,1)S(1)} %slice.36), channel_id=1, replica_groups=mesh['sess'=16,'tp'=8] {'tp'}, dimensions={1}, use_global_device_ids=true | all-gather | bytes 589824 | tf_op jit(solution)/shard_map/all_gather | solution.py:107
  253.5 0.3 reshape.256
  253.8 0.1 reshape.267
  254.0 0.5 fusion.39
  254.5 0.1 copy.25
  254.6 0.1 select_reduce_fusion.1
  254.7 0.1 fusion.52
  254.8 0.1 fusion.53
  254.9 0.1 copy.27
  255.0 0.3 reshape.255
  255.4 0.5 fusion.37
  255.9 0.1 divide_convert_fusion.2
  256.0 0.1 convert_element_type.66
  256.1 0.0 copy-done
  256.1 0.0 copy-done.4
  256.2 1.0 fusion.30
  (15 shorter events, 0.1 us)
Async XLA Ops:
  6.5 249.6 %copy-start = (bf16[1,1024,1024]{2,1,0:T(8,128)(2,1)S(1)}, bf16[1,1024,1024]{2,1,0:T(8,128)(2,1)}, u32[]{:S(2)}) copy-start(bf16[1,1024,1024]{2,1,0:T(8,128)(2,1)} %param.23) | copy-start | bytes 6291460
  6.5 117.3 %all-reduce.2.cloned.1.call-start = ((), (), s32[]{:S(2)}) async-start(), calls=%async_computation.1 | async-start | bytes 1048576 | tf_op jit(solution)/shard_map/psum | solution.py:75
  9.0 29.4 %copy-start.3 = (bf16[1024,512]{1,0:T(8,128)(2,1)S(1)}, bf16[1024,512]{1,0:T(8,128)(2,1)}, u32[]{:S(2)}) copy-start(bf16[1024,512]{1,0:T(8,128)(2,1)} %param.16) | copy-start | bytes 3145732
  12.6 27.2 %copy-start.7 = (s32[256,1]{0,1:T(1,128)S(1)}, s32[256,1]{0,1:T(1,128)}, u32[]{:S(2)}) copy-start(s32[256,1]{0,1:T(1,128)} %param.20) | copy-start | bytes 3076
  12.6 111.2 %copy-start.2 = (bf16[256,512]{1,0:T(8,128)(2,1)S(1)}, bf16[256,512]{1,0:T(8,128)(2,1)}, u32[]{:S(2)}) copy-start(bf16[256,512]{1,0:T(8,128)(2,1)} %param.12) | copy-start | bytes 786436
  12.6 139.6 %copy-start.1 = (bf16[1,512,1024]{2,1,0:T(8,128)(2,1)S(1)}, bf16[1,512,1024]{2,1,0:T(8,128)(2,1)}, u32[]{:S(2)}) copy-start(bf16[1,512,1024]{2,1,0:T(8,128)(2,1)} %param.18) | copy-start | bytes 3145732
  12.6 139.6 %copy-start.6 = (f32[512]{0:T(512)S(1)}, f32[512]{0:T(512)}, u32[]{:S(2)}) copy-start(f32[512]{0:T(512)} %param.17) | copy-start | bytes 6148
  16.0 198.4 %copy-start.5 = (f32[1,1024]{1,0:T(1,128)S(1)}, f32[1,1024]{1,0:T(1,128)}, u32[]{:S(2)}) copy-start(f32[1,1024]{1,0:T(1,128)} %param.21) | copy-start | bytes 12292
  39.7 173.6 %reduce-scatter.2.cloned.1.call-start = ((), (), s32[]{:S(2)}) async-start(), calls=%async_computation.2 | async-start | bytes 1114112 | tf_op jit(solution)/shard_map/reduce_scatter | solution.py:87
  214.3 41.8 %copy-start.4 = (f32[16,1024]{1,0:T(8,128)S(1)}, f32[16,1024]{1,0:T(8,128)}, u32[]{:S(2)}) copy-start(f32[16,1024]{1,0:T(8,128)} %reduce-scatter.2.cloned.1.call-done) | copy-start | bytes 196612
Sparse Core Ops, SparseCore 0:
  39.9 83.8 all-reduce.1
  156.1 57.2 reduce-scatter.1
where the time goes:
time: 264 us
  waiting for transfers between devices  141 us (53%)
  blocking collectives  84.9 us (32%)
  matrix products  17.6 us (7%)
  between operations  13.6 us (5%)
  other arithmetic  4.31 us (2%)
    psum x1, waiting for transfers between devices, shards(): summed = lax.psum(partial_out, 'tp')  84 us
    reduce_scatter x1, waiting for transfers between devices, shards(): lax.psum_scatter((projected + looked).reshape(sess_rows * lax.axis_size('...  57.4 us
    all_gather x1, blocking collectives, shards(): block_in = lax.all_gather(key_values, 'tp', axis=1, tiled=True)  35.2 us
    psum x1, blocking collectives, shards(): squares = lax.psum(jnp.sum(hidden * hidden, axis=1), 'sess')  27.1 us
    all_gather x1, blocking collectives, shards(): lax.all_gather(attn_rows, 'sess', axis=0, tiled=True)  22.5 us
  transfers between devices with their start and end apart: 2, of which 2 were waited for; matrix products, arithmetic and copies ran while one was open for 0% of the time, Pallas kernels for 0%

commit v1 on v0

v1 whole, which is shorter than its diff:
```python
import jax
import jax.numpy as jnp
from jax import lax
from jax.experimental import pallas as pl
from jax.experimental.pallas import tpu as pltpu
from jax.sharding import PartitionSpec as P

MESH = pl.DeviceIdType.MESH
F32 = jnp.float32
BF16 = jnp.bfloat16

D = 8192
EPS = 1e-05
CHIPS = 8
TP = 8
ROWS = 16
GROUP = 8
HD = 128
FRAMES = 1024
COLS = 512
DDEP = 1024
WIDE = DDEP + 128
PAIR = 128
DH = 64
SESS_PER_STEP = 4


def nt_dot(a, b):
    return lax.dot_general(a, b, (((1,), (1,)), ((), ())), preferred_element_type=F32)


def dot(a, b):
    return jnp.dot(a, b, preferred_element_type=F32)


def frame_kernel(
    x_hbm,
    qkv_hbm,
    kv_hbm,
    lens_hbm,
    wo_hbm,
    gain_hbm,
    win_hbm,
    emb_hbm,
    tok_hbm,
    dgain_hbm,
    dqkv_hbm,
    dout_hbm,
    out_ref,
    kv,
    wo,
    win,
    emb,
    dqkv,
    dout,
    xres,
    qkv,
    lens,
    gain,
    dgain,
    tok,
    kv_sem,
    in_sem,
    q_scr,
    o_scr,
    attn_all,
    part,
    part_in,
    hid_all,
    onehot,
    look_sib,
    look_in_sib,
    look_out,
    look_in,
    c_sib,
    c_in_sib,
    c_own,
    c_out,
    c_in,
    d_out,
    d_in,
    e_out,
    e_in,
    a_send,
    a_recv,
    as_send,
    as_recv,
    b_send,
    b_recv,
    h_send,
    h_recv,
    c_send,
    c_recv,
    d_send,
    d_recv,
    e_send,
    e_recv,
    l_send,
    l_recv,
    sib_send,
    sib_recv,
):
    s = lax.axis_index("sess")
    t = lax.axis_index("tp")
    chip = s // 2
    core = s % 2
    other = 1 - core
    sibling = (chip * 2 + other, t)

    def chip_at(d):
        return ((chip // 4 + d // 4) % 2) * 4 + (chip % 4 + d % 4) % 4

    def chip_from(d):
        return ((chip // 4 + d // 4) % 2) * 4 + (chip % 4 + 4 - d % 4) % 4

    def tp_at(d):
        return ((t // 4 + d // 4) % 2) * 4 + (t % 4 + d % 4) % 4

    def tp_from(d):
        return ((t // 4 + d // 4) % 2) * 4 + (t % 4 + 4 - d % 4) % 4

    def remote(src, dst, send, recv, device):
        return pltpu.make_async_remote_copy(
            src_ref=src,
            dst_ref=dst,
            send_sem=send,
            recv_sem=recv,
            device_id=device,
            device_id_type=MESH,
        )

    def load(i, src, dst):
        return pltpu.make_async_copy(src, dst, in_sem.at[i])

    x_load = load(0, x_hbm.at[pl.ds(pl.multiple_of(t * 32, 32), 32)], xres)
    qkv_load = load(1, qkv_hbm, qkv)
    lens_load = load(2, lens_hbm, lens)
    gain_load = load(3, gain_hbm, gain)
    dgain_load = load(4, dgain_hbm, dgain)
    tok_load = load(5, tok_hbm, tok)
    emb_load = load(6, emb_hbm, emb)
    wo_load = load(7, wo_hbm, wo)
    win_load = load(8, win_hbm, win)
    dqkv_load = load(9, dqkv_hbm, dqkv)
    dout_load = load(10, dout_hbm, dout)
    kv_loads = [pltpu.make_async_copy(kv_hbm.at[i], kv.at[i], kv_sem.at[i]) for i in range(ROWS)]

    qkv_load.start()
    lens_load.start()
    for copy in kv_loads[:8]:
        copy.start()
    tok_load.start()
    emb_load.start()
    for copy in kv_loads[8:]:
        copy.start()
    gain_load.start()
    dgain_load.start()
    x_load.start()

    barrier = pltpu.get_barrier_semaphore()
    pl.semaphore_signal(barrier, inc=1, device_id=sibling, device_id_type=MESH)
    for d in range(1, CHIPS):
        pl.semaphore_signal(barrier, inc=1, device_id=(chip_at(d) * 2 + core, t), device_id_type=MESH)
        pl.semaphore_signal(barrier, inc=1, device_id=(s, tp_at(d)), device_id_type=MESH)

    qkv_load.wait()
    lens_load.wait()
    for h in range(GROUP):
        q_scr[pl.ds(h, ROWS, stride=GROUP), :] = qkv[:, h * HD : (h + 1) * HD].astype(F32)
    scale = HD ** (-0.5)
    frame = lax.broadcasted_iota(jnp.int32, (GROUP, FRAMES), 1)

    def attend(i):
        q = q_scr[i * GROUP : (i + 1) * GROUP, :]
        new_key = qkv[i : i + 1, GROUP * HD : (GROUP + 1) * HD].astype(F32)
        new_value = qkv[i : i + 1, (GROUP + 1) * HD :].astype(F32)
        new_score = jnp.sum(q * new_key, axis=1, keepdims=True) * scale
        scores = nt_dot(q.astype(BF16), kv[i, 0]) * scale
        scores = jnp.where(frame < lens[i], scores, -1e30)
        peak = jnp.maximum(jnp.max(scores, axis=1, keepdims=True), new_score)
        expo = jnp.exp(scores - peak)
        new_expo = jnp.exp(new_score - peak)
        inv = 1.0 / (jnp.sum(expo, axis=1, keepdims=True) + new_expo)
        weights = (expo * inv).astype(BF16)
        new_weight = (new_expo * inv).astype(BF16).astype(F32)
        o_scr[i * GROUP : (i + 1) * GROUP, :] = dot(weights, kv[i, 1]) + new_weight * new_value

    def attend_step(g):
        for i in range(g * SESS_PER_STEP, (g + 1) * SESS_PER_STEP):
            kv_loads[i].wait()
        for i in range(g * SESS_PER_STEP, (g + 1) * SESS_PER_STEP):
            attend(i)

    attend_step(0)

    tok_load.wait()
    emb_load.wait()
    entry = lax.broadcasted_iota(jnp.int32, (128, 256), 0) + s * 128
    hot = jnp.where(tok[...] == entry, 1.0, 0.0).T.astype(BF16)
    onehot[...] = hot.reshape(CHIPS, 2, ROWS, 128)
    hot_other = onehot[:, pl.ds(other, 1)].reshape(CHIPS * ROWS, 128)
    look_sib[...] = dot(hot_other, emb[...]).astype(BF16).reshape(CHIPS, ROWS, DDEP)
    pl.semaphore_wait(barrier, 15)
    look_to_sib = remote(look_sib, look_in_sib, sib_send.at[0], sib_recv.at[0], sibling)
    look_to_sib.start()

    attend_step(1)

    hot_own = onehot[:, pl.ds(core, 1)].reshape(CHIPS * ROWS, 128)
    look_to_sib.wait()
    look_out[...] = (
        dot(hot_own, emb[...]).reshape(CHIPS, ROWS, DDEP) + look_in_sib[...].astype(F32)
    ).astype(BF16)
    look_copies = []
    for d in range(1, CHIPS):
        to = chip_at(d)
        copy = remote(look_out.at[to], look_in.at[d], l_send.at[d], l_recv.at[d], (to * 2 + core, t))
        copy.start()
        look_copies.append(copy)

    attend_step(2)
    wo_load.start()
    win_load.start()
    attend_step(3)
    dqkv_load.start()
    dout_load.start()

    for h in range(GROUP):
        attn_all[chip, core, :, h * HD : (h + 1) * HD] = o_scr[pl.ds(h, ROWS, stride=GROUP), :].astype(BF16)
    mine = attn_all.at[chip, core]
    gather = []
    for d in range(1, CHIPS):
        copy = remote(mine, mine, a_send.at[d], a_recv.at[d], (chip_at(d) * 2 + core, t))
        copy.start()
        gather.append(copy)
    across = [remote(mine, mine, as_send.at[0], as_recv.at[0], sibling)]
    across[0].start()

    gain_load.wait()
    win_load.wait()
    gain_col = jnp.broadcast_to(gain[...], (128, COLS)).T
    for j in range(DDEP // 128):
        cols = slice(j * 128, (j + 1) * 128)
        win[:, cols] = (win[:, cols].astype(F32) * gain_col).astype(BF16)

    for d in range(1, CHIPS):
        gather[d - 1].wait_recv()
        block = attn_all.at[chip_from(d), core]
        copy = remote(block, block, as_send.at[d], as_recv.at[d], sibling)
        copy.start()
        across.append(copy)
    wo_load.wait()
    for copy in across:
        copy.wait_recv()

    for q in range(2):
        rows = attn_all[q * 4 : (q + 1) * 4].reshape(128, GROUP * HD)
        part[q * 4 : (q + 1) * 4] = dot(rows, wo[...]).astype(BF16).reshape(4, 32, COLS)
    reduce_tp = []
    for d in range(1, TP):
        to = tp_at(d)
        copy = remote(part.at[to], part_in.at[d], b_send.at[d], b_recv.at[d], (s, to))
        copy.start()
        reduce_tp.append(copy)
    x_load.wait()
    hidden = xres[...].astype(F32) + part[t].astype(F32)
    for d in range(1, TP):
        reduce_tp[d - 1].wait_recv()
        hidden = hidden + part_in[d].astype(F32)
    hid_all[t] = hidden.astype(BF16).reshape(2, ROWS, COLS)
    my_hidden = hid_all.at[t]
    gather_tp = []
    for d in range(1, TP):
        copy = remote(my_hidden, my_hidden, h_send.at[d], h_recv.at[d], (s, tp_at(d)))
        copy.start()
        gather_tp.append(copy)
    for copy in gather_tp:
        copy.wait_recv()

    lane = lax.broadcasted_iota(jnp.int32, (CHIPS * ROWS, 128), 1)

    def project(parity):
        rows = hid_all[:, pl.ds(parity, 1)].reshape(CHIPS * ROWS, COLS)
        wide = rows.astype(F32)
        squares = jnp.sum(wide * wide, axis=1, keepdims=True)
        high = squares.astype(BF16).astype(F32)
        low = squares - high
        extra = jnp.where(lane == 2 * core, high, 0.0) + jnp.where(lane == 2 * core + 1, low, 0.0)
        return dot(rows, win[...]).reshape(CHIPS, ROWS, DDEP), extra.reshape(CHIPS, ROWS, 128)

    product, extra = project(other)
    c_sib[:, :, :DDEP] = product.astype(BF16)
    c_sib[:, :, DDEP:] = extra.astype(BF16)
    to_sib = remote(c_sib, c_in_sib, sib_send.at[1], sib_recv.at[1], sibling)
    to_sib.start()
    product, extra = project(core)
    c_own[:, :, :DDEP] = product
    c_own[:, :, DDEP:] = extra
    to_sib.wait()
    c_out[...] = (c_own[...] + c_in_sib[...].astype(F32)).astype(BF16)
    reduce_sess = []
    for d in range(1, CHIPS):
        to = chip_at(d)
        copy = remote(c_out.at[to], c_in.at[d], c_send.at[d], c_recv.at[d], (to * 2 + core, t))
        copy.start()
        reduce_sess.append(copy)
    looked = look_out[chip].astype(F32)
    for d in range(1, CHIPS):
        look_copies[d - 1].wait_recv()
        looked = looked + look_in[d].astype(F32)
    summed = c_out[chip].astype(F32)
    for d in range(1, CHIPS):
        reduce_sess[d - 1].wait_recv()
        summed = summed + c_in[d].astype(F32)
    squares = jnp.sum(summed[:, DDEP:], axis=1, keepdims=True)
    depth_in = summed[:, :DDEP] * lax.rsqrt(squares / D + EPS) + looked

    dgain_load.wait()
    mean_sq = jnp.mean(depth_in * depth_in, axis=1, keepdims=True)
    normed = (depth_in * lax.rsqrt(mean_sq + EPS) * dgain[...]).astype(BF16)
    dqkv_load.wait()
    for u in range(4):
        for p in range(3):
            first = p * DDEP + u * 256
            y = dot(normed, dqkv[:, first : first + 256]).astype(BF16)
            d_out[2 * u, :, p * PAIR : (p + 1) * PAIR] = y[:, :PAIR]
            d_out[2 * u + 1, :, p * PAIR : (p + 1) * PAIR] = y[:, PAIR:]
    heads_out = []
    for d in range(1, TP):
        to = tp_at(d)
        copy = remote(d_out.at[to], d_in.at[t], d_send.at[d], d_recv.at[d], (s, to))
        copy.start()
        heads_out.append(copy)
    d_in[t] = d_out[t]
    for copy in heads_out:
        copy.wait_recv()

    qs = [d_in[c, :, :PAIR].astype(F32) for c in range(TP)]
    ks = [d_in[c, :, PAIR : 2 * PAIR].astype(F32) for c in range(TP)]
    vs = [d_in[c, :, 2 * PAIR :].astype(F32) for c in range(TP)]
    products = jnp.concatenate([qs[c] * ks[j] for c in range(TP) for j in range(c + 1)], axis=0)
    high = products.astype(BF16)
    low = (products - high.astype(F32)).astype(BF16)
    half_r = lax.broadcasted_iota(jnp.int32, (PAIR, PAIR), 0) // DH
    half_c = lax.broadcasted_iota(jnp.int32, (PAIR, PAIR), 1) // DH
    same_head = jnp.where(half_r == half_c, 1.0, 0.0).astype(BF16)
    scores = (dot(high, same_head) + dot(low, same_head)) * DH ** (-0.5)
    at = 0
    for c in range(TP):
        rows = [scores[(at + j) * ROWS : (at + j + 1) * ROWS] for j in range(c + 1)]
        at += c + 1
        peak = rows[0]
        for row in rows[1:]:
            peak = jnp.maximum(peak, row)
        total = jnp.zeros((ROWS, PAIR), F32)
        context = jnp.zeros((ROWS, PAIR), F32)
        for j, row in enumerate(rows):
            weight = jnp.exp(row - peak)
            total = total + weight
            context = context + weight * vs[j]
        e_out[c] = (context / total).astype(BF16)
    heads_back = []
    for d in range(1, TP):
        to = tp_at(d)
        copy = remote(e_out.at[to], e_in.at[t], e_send.at[d], e_recv.at[d], (s, to))
        copy.start()
        heads_back.append(copy)
    e_in[t] = e_out[t]
    dout_load.wait()
    for copy in heads_back:
        copy.wait_recv()
    context = jnp.concatenate([e_in[c] for c in range(TP)], axis=1)
    out_ref[...] = (depth_in + dot(context, dout[...])).astype(BF16)

    for copy in gather + across + reduce_tp + gather_tp + reduce_sess + look_copies + heads_out + heads_back:
        copy.wait_send()


def shards(
    x_resid,
    qkv_new,
    kv_cache,
    cache_lens,
    wo_temporal,
    norm_gain,
    w_in,
    embed_rows,
    token_ids,
    depth_gain,
    depth_qkv,
    depth_out,
):
    args = (
        x_resid,
        qkv_new.reshape(ROWS, (GROUP + 2) * HD),
        kv_cache.reshape(ROWS, 2, FRAMES, HD),
        cache_lens,
        wo_temporal,
        norm_gain.reshape(1, COLS),
        w_in.reshape(COLS, DDEP),
        embed_rows.reshape(128, DDEP),
        token_ids.reshape(1, 256),
        depth_gain,
        depth_qkv.reshape(DDEP, 3 * DDEP),
        depth_out.reshape(DDEP, DDEP),
    )
    dma = pltpu.SemaphoreType.DMA
    vm = pltpu.VMEM
    out = pl.pallas_call(
        frame_kernel,
        name="frame",
        out_shape=jax.ShapeDtypeStruct((ROWS, DDEP), BF16),
        in_specs=[pl.BlockSpec(memory_space=pl.ANY)] * len(args),
        out_specs=pl.BlockSpec(memory_space=pltpu.VMEM),
        scratch_shapes=[
            vm((ROWS, 2, FRAMES, HD), BF16),
            vm((GROUP * HD, COLS), BF16),
            vm((COLS, DDEP), BF16),
            vm((128, DDEP), BF16),
            vm((DDEP, 3 * DDEP), BF16),
            vm((DDEP, DDEP), BF16),
            vm((32, COLS), BF16),
            vm((ROWS, (GROUP + 2) * HD), BF16),
            pltpu.SMEM((ROWS,), jnp.int32),
            vm((1, COLS), F32),
            vm((1, DDEP), F32),
            vm((1, 256), jnp.int32),
            dma((ROWS,)),
            dma((11,)),
            vm((ROWS * GROUP, HD), F32),
            vm((ROWS * GROUP, HD), F32),
            vm((CHIPS, 2, ROWS, GROUP * HD), BF16),
            vm((TP, 32, COLS), BF16),
            vm((TP, 32, COLS), BF16),
            vm((TP, 2, ROWS, COLS), BF16),
            vm((CHIPS, 2, ROWS, 128), BF16),
            vm((CHIPS, ROWS, DDEP), BF16),
            vm((CHIPS, ROWS, DDEP), BF16),
            vm((CHIPS, ROWS, DDEP), BF16),
            vm((CHIPS, ROWS, DDEP), BF16),
            vm((CHIPS, ROWS, WIDE), BF16),
            vm((CHIPS, ROWS, WIDE), BF16),
            vm((CHIPS, ROWS, WIDE), F32),
            vm((CHIPS, ROWS, WIDE), BF16),
            vm((CHIPS, ROWS, WIDE), BF16),
            vm((TP, ROWS, 3 * PAIR), BF16),
            vm((TP, ROWS, 3 * PAIR), BF16),
            vm((TP, ROWS, PAIR), BF16),
            vm((TP, ROWS, PAIR), BF16),
            dma((8,)),
            dma((8,)),
            dma((8,)),
            dma((8,)),
            dma((8,)),
            dma((8,)),
            dma((8,)),
            dma((8,)),
            dma((8,)),
            dma((8,)),
            dma((8,)),
            dma((8,)),
            dma((8,)),
            dma((8,)),
            dma((8,)),
            dma((8,)),
            dma((2,)),
            dma((2,)),
        ],
        compiler_params=pltpu.CompilerParams(
            collective_id=0, has_side_effects=True, vmem_limit_bytes=48 * 2**20
        ),
        cost_estimate=pl.CostEstimate(flops=10**9, bytes_accessed=19 * 10**6, transcendentals=10**5),
    )(*args)
    return out.reshape(ROWS, 1, DDEP)


def solution(mesh):
    in_specs = (
        P(None, "sess"),
        P("sess", "tp", None),
        P("sess", None, "tp", None, None),
        P("sess"),
        P("tp", "sess"),
        P("sess"),
        P("tp", "sess", None),
        P("tp", "sess", None),
        P(None, "tp"),
        P("tp", None),
        P("tp", None, None),
        P("tp", None, None),
    )
    out_specs = P("sess", "tp", None)
    return jax.shard_map(shards, mesh=mesh, in_specs=in_specs, out_specs=out_specs, check_vma=False)
```

time: 264 us -> 64.7 us (0.25)
  waiting for transfers between devices: 141 us -> 0 us
  blocking collectives: 84.9 us -> 0 us
  Pallas kernels: 0 us -> 54.2 us
  matrix products: 17.6 us -> 0 us
  between operations: 13.6 us -> 0.02 us
  local copies, waits for them, and re-layouts: 2.15 us -> 10 us
  other arithmetic: 4.31 us -> 0 us
    psum x1 -> x0, waiting for transfers between devices: 84 us -> none  [shards(): summed = lax.psum(partial_out, 'tp')]
    all_gather x2 -> x0, blocking collectives: 57.7 us -> none  [the longest x1 35.2 us: shards(): block_in = lax.all_gather(key_values, 'tp', axis=1, tiled=True)]
    reduce_scatter x1 -> x0, waiting for transfers between devices: 57.4 us -> none  [shards(): lax.psum_scatter((projected + looked).reshape(sess_rows * lax.axis_size('...]
    pallas_call x0 -> x1, Pallas kernels: none -> 54.2 us  [shards(): pl.pallas_call(frame_kernel, name='frame', out_shape=jax.ShapeDtypeStruct...]
    psum x1 -> x0, blocking collectives: 27.1 us -> none  [shards(): squares = lax.psum(jnp.sum(hidden * hidden, axis=1), 'sess')]
    dot_general x10 -> x0, matrix products: 17.6 us -> none  [the longest x1 3.82 us: shards(): jnp.einsum('sce,cef->scf', depth_normed, depth_qkv, preferred_element_typ...]
    unnamed x19 -> x21, local copies, waits for them, and re-layouts: 0.97 us -> 10 us
  transfers between devices with their start and end apart: 2 -> 0, of which waited for: 2 -> 0; matrix products, arithmetic and copies ran while one was open for 0% -> 0% of each run, Pallas kernels for 0% -> 0%
where the time goes in v1:
time: 64.7 us; the launch traced here: 64.3 us
  Pallas kernels  54.2 us (84%)
  local copies, waits for them, and re-layouts  10 us (15%)
    pallas_call x1, Pallas kernels, shards(): pl.pallas_call(frame_kernel, name='frame', out_shape=jax.ShapeDtypeStruct...  54.2 us
    unnamed x21, local copies, waits for them, and re-layouts  10 us

profile of v1, /device:TPU:0, one launch (start us, length us, event | category | flops | bytes accessed | tf_op | source)
XLA Modules:
  0.0 64.3 jit_solution(11924020139438056787)
XLA Ops:
  0.0 0.0 copy-start
  0.0 1.6 %copy-done = bf16[1,1024,1024]{2,1,0:T(8,128)(2,1)S(1)} copy-done((bf16[1,1024,1024]{2,1,0:T(8,128)(2,1)S(1)}, bf16[1,1024,1024]{2,1,0:T(8,128)(2,1)}, u32[]{:S(2)}) %copy-start) | copy-done | bytes 2097176
  1.6 0.0 copy-start.1
  1.6 1.2 %copy-done.1 = bf16[1024,512]{1,0:T(8,128)(2,1)S(1)} copy-done((bf16[1024,512]{1,0:T(8,128)(2,1)S(1)}, bf16[1024,512]{1,0:T(8,128)(2,1)}, u32[]{:S(2)}) %copy-start.1) | copy-done | bytes 1048600
  2.8 0.0 copy-start.2
  2.8 1.2 %copy-done.2 = bf16[1,512,1024]{2,1,0:T(8,128)(2,1)S(1)} copy-done((bf16[1,512,1024]{2,1,0:T(8,128)(2,1)S(1)}, bf16[1,512,1024]{2,1,0:T(8,128)(2,1)}, u32[]{:S(2)}) %copy-start.2) | copy-done | bytes 1048600
  4.0 0.0 copy-start.3
  4.0 0.9 %copy-done.3 = bf16[256,512]{1,0:T(8,128)(2,1)S(1)} copy-done((bf16[256,512]{1,0:T(8,128)(2,1)S(1)}, bf16[256,512]{1,0:T(8,128)(2,1)}, u32[]{:S(2)}) %copy-start.3) | copy-done | bytes 262168
  5.0 0.0 copy-start.4
  5.0 0.9 %copy-done.4 = bf16[1,128,1024]{2,1,0:T(8,128)(2,1)S(1)} copy-done((bf16[1,128,1024]{2,1,0:T(8,128)(2,1)S(1)}, bf16[1,128,1024]{2,1,0:T(8,128)(2,1)}, u32[]{:S(2)}) %copy-start.4) | copy-done | bytes 262168
  5.9 0.0 copy-start.5
  5.9 0.8 %copy-done.5 = bf16[16,1,1280]{2,0,1:T(8,128)(2,1)S(1)} copy-done((bf16[16,1,1280]{2,0,1:T(8,128)(2,1)S(1)}, bf16[16,1,1280]{2,0,1:T(8,128)(2,1)}, u32[]{:S(2)}) %copy-start.5) | copy-done | bytes 40984
  6.7 0.0 copy-start.6
  6.7 0.7 %copy-done.6 = f32[1,1024]{1,0:T(1,128)S(1)} copy-done((f32[1,1024]{1,0:T(1,128)S(1)}, f32[1,1024]{1,0:T(1,128)}, u32[]{:S(2)}) %copy-start.6) | copy-done | bytes 4120
  7.4 0.0 copy-start.7
  7.4 0.7 %copy-done.7 = f32[512]{0:T(512)S(1)} copy-done((f32[512]{0:T(512)S(1)}, f32[512]{0:T(512)}, u32[]{:S(2)}) %copy-start.7) | copy-done | bytes 2072
  8.1 0.0 copy-start.8
  8.1 0.7 %copy-done.8 = s32[256,1]{0,1:T(1,128)S(1)} copy-done((s32[256,1]{0,1:T(1,128)S(1)}, s32[256,1]{0,1:T(1,128)}, u32[]{:S(2)}) %copy-start.8) | copy-done | bytes 1048
  8.8 0.0 copy-start.9
  8.8 0.7 %copy-done.9 = s32[16]{0:T(128)S(1)} copy-done((s32[16]{0:T(128)S(1)}, s32[16]{0:T(128)}, u32[]{:S(2)}) %copy-start.9) | copy-done | bytes 88
  9.4 54.2 %frame.1 = bf16[16,1024]{1,0:T(8,128)(2,1)S(1)} custom-call(bf16[256,512]{1,0:T(8,128)(2,1)S(1)} %copy-done.3, bf16[16,1280]{1,0:T(8,128)(2,1)S(1)} %bitcast.13, bf16[16,2,1024,128]{3,2,1,0:T(8,128)(2,1)} %bitcast.16, s32[16]{0:T(128)S(1)} %copy-done.9, bf16[1024,512]{1,0:T(8,128)(2,1)S(1)} %copy-done.1, f32[1,512]{1,0:T(1,128)S(1)} %bitcast.14, ...), custom_call_target="tpu_custom_call" | custom-call | flops 1000000000 | bytes 19000000 | tf_op jit(solution)/shard_map/frame/pallas_call | solution.py:409
  63.6 0.6 copy.14
Async XLA Ops:
  0.0 1.6 %copy-start = (bf16[1,1024,1024]{2,1,0:T(8,128)(2,1)S(1)}, bf16[1,1024,1024]{2,1,0:T(8,128)(2,1)}, u32[]{:S(2)}) copy-start(bf16[1,1024,1024]{2,1,0:T(8,128)(2,1)} %param.23) | copy-start | bytes 6291460
  1.6 1.2 %copy-start.1 = (bf16[1024,512]{1,0:T(8,128)(2,1)S(1)}, bf16[1024,512]{1,0:T(8,128)(2,1)}, u32[]{:S(2)}) copy-start(bf16[1024,512]{1,0:T(8,128)(2,1)} %wo_hbm.1) | copy-start | bytes 3145732
  2.8 1.2 %copy-start.2 = (bf16[1,512,1024]{2,1,0:T(8,128)(2,1)S(1)}, bf16[1,512,1024]{2,1,0:T(8,128)(2,1)}, u32[]{:S(2)}) copy-start(bf16[1,512,1024]{2,1,0:T(8,128)(2,1)} %param.18) | copy-start | bytes 3145732
  4.0 0.9 %copy-start.3 = (bf16[256,512]{1,0:T(8,128)(2,1)S(1)}, bf16[256,512]{1,0:T(8,128)(2,1)}, u32[]{:S(2)}) copy-start(bf16[256,512]{1,0:T(8,128)(2,1)} %x_hbm.1) | copy-start | bytes 786436
  5.0 0.9 %copy-start.4 = (bf16[1,128,1024]{2,1,0:T(8,128)(2,1)S(1)}, bf16[1,128,1024]{2,1,0:T(8,128)(2,1)}, u32[]{:S(2)}) copy-start(bf16[1,128,1024]{2,1,0:T(8,128)(2,1)} %param.19) | copy-start | bytes 786436
  5.9 0.8 %copy-start.5 = (bf16[16,1,1280]{2,0,1:T(8,128)(2,1)S(1)}, bf16[16,1,1280]{2,0,1:T(8,128)(2,1)}, u32[]{:S(2)}) copy-start(bf16[16,1,1280]{2,0,1:T(8,128)(2,1)} %param.13) | copy-start | bytes 122884
  6.7 0.7 %copy-start.6 = (f32[1,1024]{1,0:T(1,128)S(1)}, f32[1,1024]{1,0:T(1,128)}, u32[]{:S(2)}) copy-start(f32[1,1024]{1,0:T(1,128)} %dgain_hbm.1) | copy-start | bytes 12292
  7.4 0.7 %copy-start.7 = (f32[512]{0:T(512)S(1)}, f32[512]{0:T(512)}, u32[]{:S(2)}) copy-start(f32[512]{0:T(512)} %param.17) | copy-start | bytes 6148
  8.1 0.7 %copy-start.8 = (s32[256,1]{0,1:T(1,128)S(1)}, s32[256,1]{0,1:T(1,128)}, u32[]{:S(2)}) copy-start(s32[256,1]{0,1:T(1,128)} %param.20) | copy-start | bytes 3076
  8.8 0.7 %copy-start.9 = (s32[16]{0:T(128)S(1)}, s32[16]{0:T(128)}, u32[]{:S(2)}) copy-start(s32[16]{0:T(128)} %lens_hbm.1) | copy-start | bytes 196

commit v2 on v1

v2 whole, which is shorter than its diff:
```python
import jax
import jax.numpy as jnp
from jax import lax
from jax.experimental import pallas as pl
from jax.experimental.pallas import tpu as pltpu
from jax.sharding import PartitionSpec as P

MESH = pl.DeviceIdType.MESH
F32 = jnp.float32
BF16 = jnp.bfloat16

D = 8192
EPS = 1e-05
CHIPS = 8
TP = 8
ROWS = 16
GROUP = 8
HD = 128
FRAMES = 1024
COLS = 512
DDEP = 1024
WIDE = DDEP + 128
QUAD = 256
DH = 64
STEP = 4


def dot(a, b):
    return jnp.dot(a, b, preferred_element_type=F32)


def frame_kernel(
    x_hbm,
    qkv_hbm,
    kv_hbm,
    lens_hbm,
    wo_hbm,
    gain_hbm,
    win_hbm,
    emb_hbm,
    tok_hbm,
    dgain_hbm,
    dqkv_hbm,
    dout_hbm,
    out_ref,
    keys,
    values,
    wo,
    win,
    emb,
    dqkv,
    dout,
    xres,
    qkv,
    lens,
    gain,
    dgain,
    tok,
    kv_sem,
    in_sem,
    q_scr,
    k_scr,
    v_scr,
    query_cols,
    score_scr,
    weight_scr,
    o_scr,
    attn_all,
    part,
    part_in,
    hid_all,
    onehot,
    look_own,
    look_sib,
    look_in_sib,
    look_out,
    look_in,
    c_sib,
    c_in_sib,
    c_out,
    c_in,
    d_out,
    d_in,
    e_out,
    e_in,
    a_send,
    a_recv,
    f_send,
    f_recv,
    b_send,
    b_recv,
    h_send,
    h_recv,
    c_send,
    c_recv,
    d_send,
    d_recv,
    e_send,
    e_recv,
    l_send,
    l_recv,
    sib_send,
    sib_recv,
):
    s = lax.axis_index("sess")
    t = lax.axis_index("tp")
    chip = s // 2
    core = s % 2
    other = 1 - core
    row = t // 4
    col = t % 4
    sibling = (chip * 2 + other, t)

    def step_of(d):
        return ((0, 1), (0, 3), (1, 0), (0, 2), (1, 1), (1, 3), (1, 2))[d - 1]

    def at(i, d):
        hi, lo = step_of(d)
        return ((i // 4 + hi) % 2) * 4 + (i % 4 + lo) % 4

    def back(i, d):
        hi, lo = step_of(d)
        return ((i // 4 + hi) % 2) * 4 + (i % 4 + 4 - lo) % 4

    far_first = (7, 6, 5, 4, 3, 2, 1)
    near_first = (1, 2, 3, 4, 5, 6, 7)

    def remote(src, dst, send, recv, device):
        return pltpu.make_async_remote_copy(
            src_ref=src,
            dst_ref=dst,
            send_sem=send,
            recv_sem=recv,
            device_id=device,
            device_id_type=MESH,
        )

    def load(i, src, dst):
        return pltpu.make_async_copy(src, dst, in_sem.at[i])

    x_load = load(0, x_hbm.at[pl.ds(pl.multiple_of(t * 32, 32), 32)], xres)
    qkv_load = load(1, qkv_hbm, qkv)
    lens_load = load(2, lens_hbm, lens)
    gain_load = load(3, gain_hbm, gain)
    dgain_load = load(4, dgain_hbm, dgain)
    tok_load = load(5, tok_hbm, tok)
    emb_load = load(6, emb_hbm, emb)
    wo_load = load(7, wo_hbm, wo)
    win_load = load(8, win_hbm, win)
    dqkv_load = load(9, dqkv_hbm, dqkv)
    dout_load = load(10, dout_hbm, dout)
    key_loads = [
        pltpu.make_async_copy(kv_hbm.at[pl.ds(g * STEP, STEP), 0], keys.at[pl.ds(g * STEP, STEP)], kv_sem.at[0, g])
        for g in range(ROWS // STEP)
    ]
    value_loads = [
        pltpu.make_async_copy(kv_hbm.at[pl.ds(g * STEP, STEP), 1], values.at[pl.ds(g * STEP, STEP)], kv_sem.at[1, g])
        for g in range(ROWS // STEP)
    ]
    for copy in [qkv_load, lens_load, tok_load, emb_load] + key_loads + value_loads:
        copy.start()
    for copy in (gain_load, dgain_load, x_load):
        copy.start()

    barrier = pltpu.get_barrier_semaphore()
    pl.semaphore_signal(barrier, inc=1, device_id=sibling, device_id_type=MESH)
    for d in near_first:
        for device in ((at(chip, d) * 2, t), (at(chip, d) * 2 + 1, t), (s, at(t, d))):
            pl.semaphore_signal(barrier, inc=1, device_id=device, device_id_type=MESH)

    qkv_load.wait()
    new_keys = qkv[:, GROUP * HD : (GROUP + 1) * HD].astype(F32)
    new_values = qkv[:, (GROUP + 1) * HD :].astype(F32)
    for h in range(GROUP):
        rows_h = pl.ds(h, ROWS, stride=GROUP)
        q_scr[rows_h, :] = qkv[:, h * HD : (h + 1) * HD].astype(F32)
        k_scr[rows_h, :] = new_keys
        v_scr[rows_h, :] = new_values
    query_t = q_scr[...].T
    scale = HD ** (-0.5)
    new_score = jnp.sum(query_t * k_scr[...].T, axis=0, keepdims=True) * scale
    owner = lax.broadcasted_iota(jnp.int32, (HD, HD), 1) // GROUP
    for i in range(ROWS):
        query_cols[i * HD : (i + 1) * HD, :] = jnp.where(owner == i, query_t, 0.0).astype(BF16)
    lens_load.wait()
    owner_row = lax.broadcasted_iota(jnp.int32, (1, HD), 1) // GROUP
    live = jnp.zeros((1, HD), jnp.int32)
    for i in range(ROWS):
        live = jnp.where(owner_row == i, lens[i], live)

    tok_load.wait()
    emb_load.wait()
    entry = lax.broadcasted_iota(jnp.int32, (128, 256), 0) + s * 128
    hot = jnp.where(tok[...] == entry, 1.0, 0.0).T.astype(BF16)
    onehot[...] = hot.reshape(CHIPS, 2, ROWS, 128)

    def look(parity):
        rows = onehot[:, pl.ds(parity, 1)].reshape(CHIPS * ROWS, 128)
        return dot(rows, emb[...]).astype(BF16).reshape(CHIPS, ROWS, DDEP)

    look_sib[...] = look(other)
    look_own[...] = look(core)

    for g in range(ROWS // STEP):
        key_loads[g].wait()
        joined = jnp.concatenate([keys[g * STEP + i] for i in range(STEP)], axis=1)
        scores = dot(joined, query_cols[g * STEP * HD : (g + 1) * STEP * HD, :])
        if g == 0:
            score_scr[...] = scores
        else:
            score_scr[...] += scores
    wo_load.start()
    win_load.start()
    pl.semaphore_wait(barrier, 22)
    look_to_sib = remote(look_sib, look_in_sib, sib_send.at[0], sib_recv.at[0], sibling)
    look_to_sib.start()

    frame = lax.broadcasted_iota(jnp.int32, (FRAMES, HD), 0)
    masked = jnp.where(frame < live, score_scr[...] * scale, -1e30)
    peak = jnp.maximum(jnp.max(masked, axis=0, keepdims=True), new_score)
    expo = jnp.exp(masked - peak)
    new_expo = jnp.exp(new_score - peak)
    inv = 1.0 / (jnp.sum(expo, axis=0, keepdims=True) + new_expo)
    weight_scr[...] = (expo * inv).T
    new_weight = (new_expo * inv).astype(BF16).astype(F32)
    o_scr[...] = jnp.broadcast_to(new_weight, (HD, HD)).T * v_scr[...]
    for g in range(ROWS // STEP):
        value_loads[g].wait()
        for i in range(g * STEP, (g + 1) * STEP):
            rows_i = slice(i * GROUP, (i + 1) * GROUP)
            o_scr[rows_i, :] += dot(weight_scr[rows_i, :].astype(BF16), values[i])
    dqkv_load.start()
    dout_load.start()

    for h in range(GROUP):
        attn_all[chip, core, :, h * HD : (h + 1) * HD] = o_scr[pl.ds(h, ROWS, stride=GROUP), :].astype(BF16)
    mine = attn_all.at[chip, core]
    gather = {}
    for d in far_first:
        gather[d] = remote(mine, mine, a_send.at[d], a_recv.at[d], (at(chip, d) * 2 + other, t))
        gather[d].start()
        if d == 7:
            far = remote(mine, mine, f_send.at[d], f_recv.at[d], (at(chip, d) * 2 + core, t))
            far.start()
    swap = remote(mine, mine, f_send.at[0], f_recv.at[0], sibling)
    swap.start()

    gain_load.wait()
    win_load.wait()
    gain_col = jnp.broadcast_to(gain[...], (128, COLS)).T
    for j in range(DDEP // 128):
        cols = slice(j * 128, (j + 1) * 128)
        win[:, cols] = (win[:, cols].astype(F32) * gain_col).astype(BF16)
    look_to_sib.wait()
    look_out[...] = (look_own[...].astype(F32) + look_in_sib[...].astype(F32)).astype(BF16)

    across = [far]
    for d in near_first:
        gather[d].wait_recv()
        if d < 7:
            block = attn_all.at[back(chip, d), other]
            copy = remote(block, block, f_send.at[d], f_recv.at[d], sibling)
            copy.start()
            across.append(copy)
    swap.wait_recv()
    wo_load.wait()

    reduce_tp = [{}, {}]

    def reduce_start(half, parity):
        rows = attn_all[:, pl.ds(parity, 1)].reshape(CHIPS * ROWS, GROUP * HD)
        part[half] = dot(rows, wo[...]).astype(BF16).reshape(CHIPS, ROWS, COLS)
        for d in far_first:
            to = at(t, d)
            copy = remote(part.at[half, to], part_in.at[half, d], b_send.at[half, d], b_recv.at[half, d], (s, to))
            copy.start()
            reduce_tp[half][d] = copy

    reduce_start(0, other)
    for copy in across:
        copy.wait_recv()
    reduce_start(1, core)
    look_copies = []
    for d in far_first:
        to = at(chip, d)
        copy = remote(look_out.at[to], look_in.at[d], l_send.at[d], l_recv.at[d], (to * 2 + core, t))
        copy.start()
        look_copies.append(copy)
    x_load.wait()
    gather_tp = [[], []]

    def gather_start(half, parity):
        hidden = xres[pl.ds(pl.multiple_of(parity * ROWS, ROWS), ROWS)].astype(F32) + part[half, t].astype(F32)
        for d in near_first:
            reduce_tp[half][d].wait_recv()
            hidden = hidden + part_in[half, d].astype(F32)
        hid_all[t, parity] = hidden.astype(BF16)
        block = hid_all.at[t, parity]
        for d in far_first:
            copy = remote(block, block, h_send.at[half, d], h_recv.at[half, d], (s, at(t, d)))
            copy.start()
            gather_tp[half].append(copy)

    gather_start(0, other)
    gather_start(1, core)

    lane = lax.broadcasted_iota(jnp.int32, (CHIPS * ROWS, 128), 1)

    def project(parity):
        rows = hid_all[:, pl.ds(parity, 1)].reshape(CHIPS * ROWS, COLS)
        wide = rows.astype(F32)
        squares = jnp.sum(wide * wide, axis=1, keepdims=True)
        high = squares.astype(BF16).astype(F32)
        low = squares - high
        extra = jnp.where(lane == 2 * core, high, 0.0) + jnp.where(lane == 2 * core + 1, low, 0.0)
        return dot(rows, win[...]).reshape(CHIPS, ROWS, DDEP), extra.reshape(CHIPS, ROWS, 128)

    for copy in gather_tp[0]:
        copy.wait_recv()
    product, extra = project(other)
    c_sib[:, :, :DDEP] = product.astype(BF16)
    c_sib[:, :, DDEP:] = extra.astype(BF16)
    to_sib = remote(c_sib, c_in_sib, sib_send.at[1], sib_recv.at[1], sibling)
    to_sib.start()
    looked = look_out[chip].astype(F32)
    for d in range(1, CHIPS):
        look_copies[7 - d].wait_recv()
        looked = looked + look_in[d].astype(F32)
    for copy in gather_tp[1]:
        copy.wait_recv()
    to_sib.wait()
    product, extra = project(core)
    c_out[:, :, :DDEP] = (product + c_in_sib[:, :, :DDEP].astype(F32)).astype(BF16)
    c_out[:, :, DDEP:] = (extra + c_in_sib[:, :, DDEP:].astype(F32)).astype(BF16)
    reduce_sess = {}
    for d in far_first:
        to = at(chip, d)
        copy = remote(c_out.at[to], c_in.at[d], c_send.at[d], c_recv.at[d], (to * 2 + core, t))
        copy.start()
        reduce_sess[d] = copy
    summed = c_out[chip].astype(F32)
    for d in near_first:
        reduce_sess[d].wait_recv()
        summed = summed + c_in[d].astype(F32)
    squares = jnp.sum(summed[:, DDEP:], axis=1, keepdims=True)
    depth_in = summed[:, :DDEP] * lax.rsqrt(squares / D + EPS) + looked

    dgain_load.wait()
    mean_sq = jnp.mean(depth_in * depth_in, axis=1, keepdims=True)
    normed = (depth_in * lax.rsqrt(mean_sq + EPS) * dgain[...]).astype(BF16)
    dqkv_load.wait()
    for u in range(4):
        for p in range(3):
            first = p * DDEP + u * QUAD
            d_out[u, :, p * QUAD : (p + 1) * QUAD] = dot(normed, dqkv[:, first : first + QUAD]).astype(BF16)
    down = []
    for e in (2, 1, 3, 0):
        to = (col + e) % 4
        source = d_out.at[to, :, QUAD:]
        down.append(
            remote(source, d_in.at[t, :, QUAD:], d_send.at[4 + e], d_recv.at[4 + e], (s, 4 + to))
        )

    @pl.when(row == 0)
    def _():
        for copy in down:
            copy.start()

    heads_out = []
    for e in (2, 1, 3):
        to = (col + e) % 4
        copy = remote(d_out.at[to], d_in.at[t], d_send.at[e], d_recv.at[e], (s, row * 4 + to))
        copy.start()
        heads_out.append(copy)
    d_in[t] = d_out[col]
    for copy in heads_out:
        copy.wait_recv()

    head_r = lax.broadcasted_iota(jnp.int32, (QUAD, QUAD), 0) // DH
    head_c = lax.broadcasted_iota(jnp.int32, (QUAD, QUAD), 1) // DH
    same_head = jnp.where(head_r == head_c, 1.0, 0.0).astype(BF16)

    def attend(codebooks):
        count = codebooks[-1] + 1
        qs = [d_in[c, :, :QUAD].astype(F32) for c in codebooks]
        ks = [d_in[c, :, QUAD : 2 * QUAD].astype(F32) for c in range(count)]
        vs = [d_in[c, :, 2 * QUAD :].astype(F32) for c in range(count)]
        products = jnp.concatenate(
            [qs[i] * ks[j] for i, c in enumerate(codebooks) for j in range(c + 1)], axis=0
        )
        high = products.astype(BF16)
        low = (products - high.astype(F32)).astype(BF16)
        scores = (dot(high, same_head) + dot(low, same_head)) * DH ** (-0.5)
        start = 0
        for i, c in enumerate(codebooks):
            lines = [scores[(start + j) * ROWS : (start + j + 1) * ROWS] for j in range(c + 1)]
            start += c + 1
            top = lines[0]
            for line in lines[1:]:
                top = jnp.maximum(top, line)
            total = jnp.zeros((ROWS, QUAD), F32)
            context = jnp.zeros((ROWS, QUAD), F32)
            for j, line in enumerate(lines):
                weight = jnp.exp(line - top)
                total = total + weight
                context = context + weight * vs[j]
            e_out[i] = (context / total).astype(BF16)

    @pl.when(row == 0)
    def _():
        attend((0, 1, 2, 3))

    @pl.when(row == 1)
    def _():
        for copy in down:
            copy.wait_recv()
        attend((4, 5, 6, 7))

    heads_back = []
    for e in (2, 1, 3):
        to = (col + e) % 4
        copy = remote(e_out.at[to], e_in.at[col], e_send.at[e], e_recv.at[e], (s, row * 4 + to))
        copy.start()
        heads_back.append(copy)
    e_in[col] = e_out[col]
    dout_load.wait()
    for copy in heads_back:
        copy.wait_recv()
    context = jnp.concatenate([e_in[i] for i in range(4)], axis=1)
    out_ref[...] = (depth_in + dot(context, dout[...])).astype(BF16)

    sent = list(gather.values()) + across + [swap] + gather_tp[0] + gather_tp[1] + look_copies + heads_out + heads_back
    for copies in (reduce_tp[0], reduce_tp[1], reduce_sess):
        sent += list(copies.values())
    for copy in sent:
        copy.wait_send()

    @pl.when(row == 0)
    def _():
        for copy in down:
            copy.wait_send()


def shards(
    x_resid,
    qkv_new,
    kv_cache,
    cache_lens,
    wo_temporal,
    norm_gain,
    w_in,
    embed_rows,
    token_ids,
    depth_gain,
    depth_qkv,
    depth_out,
):
    args = (
        x_resid,
        qkv_new.reshape(ROWS, (GROUP + 2) * HD),
        kv_cache.reshape(ROWS, 2, FRAMES, HD),
        cache_lens,
        wo_temporal,
        norm_gain.reshape(1, COLS),
        w_in.reshape(COLS, DDEP),
        embed_rows.reshape(128, DDEP),
        token_ids.reshape(1, 256),
        depth_gain,
        depth_qkv.reshape(DDEP, 3 * DDEP),
        depth_out.reshape(DDEP, DDEP),
    )
    args = tuple(pltpu.with_memory_space_constraint(a, pltpu.HBM) for a in args)
    dma = pltpu.SemaphoreType.DMA
    vm = pltpu.VMEM
    out = pl.pallas_call(
        frame_kernel,
        name="frame",
        out_shape=jax.ShapeDtypeStruct((ROWS, DDEP), BF16),
        in_specs=[pl.BlockSpec(memory_space=pltpu.HBM)] * len(args),
        out_specs=pl.BlockSpec(memory_space=pltpu.VMEM),
        scratch_shapes=[
            vm((ROWS, FRAMES, HD), BF16),
            vm((ROWS, FRAMES, HD), BF16),
            vm((GROUP * HD, COLS), BF16),
            vm((COLS, DDEP), BF16),
            vm((128, DDEP), BF16),
            vm((DDEP, 3 * DDEP), BF16),
            vm((DDEP, DDEP), BF16),
            vm((32, COLS), BF16),
            vm((ROWS, (GROUP + 2) * HD), BF16),
            pltpu.SMEM((ROWS,), jnp.int32),
            vm((1, COLS), F32),
            vm((1, DDEP), F32),
            vm((1, 256), jnp.int32),
            dma((2, ROWS // STEP)),
            dma((11,)),
            vm((ROWS * GROUP, HD), F32),
            vm((ROWS * GROUP, HD), F32),
            vm((ROWS * GROUP, HD), F32),
            vm((ROWS * HD, HD), BF16),
            vm((FRAMES, HD), F32),
            vm((ROWS * GROUP, FRAMES), F32),
            vm((ROWS * GROUP, HD), F32),
            vm((CHIPS, 2, ROWS, GROUP * HD), BF16),
            vm((2, TP, ROWS, COLS), BF16),
            vm((2, TP, ROWS, COLS), BF16),
            vm((TP, 2, ROWS, COLS), BF16),
            vm((CHIPS, 2, ROWS, 128), BF16),
            vm((CHIPS, ROWS, DDEP), BF16),
            vm((CHIPS, ROWS, DDEP), BF16),
            vm((CHIPS, ROWS, DDEP), BF16),
            vm((CHIPS, ROWS, DDEP), BF16),
            vm((CHIPS, ROWS, DDEP), BF16),
            vm((CHIPS, ROWS, WIDE), BF16),
            vm((CHIPS, ROWS, WIDE), BF16),
            vm((CHIPS, ROWS, WIDE), BF16),
            vm((CHIPS, ROWS, WIDE), BF16),
            vm((4, ROWS, 3 * QUAD), BF16),
            vm((TP, ROWS, 3 * QUAD), BF16),
            vm((4, ROWS, QUAD), BF16),
            vm((4, ROWS, QUAD), BF16),
            dma((8,)),
            dma((8,)),
            dma((8,)),
            dma((8,)),
            dma((2, 8)),
            dma((2, 8)),
            dma((2, 8)),
            dma((2, 8)),
            dma((8,)),
            dma((8,)),
            dma((8,)),
            dma((8,)),
            dma((4,)),
            dma((4,)),
            dma((8,)),
            dma((8,)),
            dma((2,)),
            dma((2,)),
        ],
        compiler_params=pltpu.CompilerParams(
            collective_id=0, has_side_effects=True, vmem_limit_bytes=62 * 2**20
        ),
        cost_estimate=pl.CostEstimate(flops=10**9, bytes_accessed=19 * 10**6, transcendentals=10**5),
    )(*args)
    return out.reshape(ROWS, 1, DDEP)


def solution(mesh):
    in_specs = (
        P(None, "sess"),
        P("sess", "tp", None),
        P("sess", None, "tp", None, None),
        P("sess"),
        P("tp", "sess"),
        P("sess"),
        P("tp", "sess", None),
        P("tp", "sess", None),
        P(None, "tp"),
        P("tp", None),
        P("tp", None, None),
        P("tp", None, None),
    )
    out_specs = P("sess", "tp", None)
    return jax.shard_map(shards, mesh=mesh, in_specs=in_specs, out_specs=out_specs, check_vma=False)
```

time: 64.7 us -> 49.5 us (0.77)
  local copies, waits for them, and re-layouts: 10 us -> 1.38 us
  Pallas kernels: 54.2 us -> 48 us
    unnamed x21 -> x1, local copies, waits for them, and re-layouts: 10 us -> 1.38 us
    pallas_call x1, Pallas kernels: 54.2 us -> 48 us  [shards(): pl.pallas_call(frame_kernel, name='frame', out_shape=jax.ShapeDtypeStruct...]
where the time goes in v2:
time: 49.5 us; the launch traced here: 49.4 us
  Pallas kernels  48 us (97%)
  local copies, waits for them, and re-layouts  1.38 us (3%)
    pallas_call x1, Pallas kernels, shards(): pl.pallas_call(frame_kernel, name='frame', out_shape=jax.ShapeDtypeStruct...  48 us
    unnamed x1, local copies, waits for them, and re-layouts  1.38 us

profile of v2, /device:TPU:0, one launch (start us, length us, event | category | flops | bytes accessed | tf_op | source)
XLA Modules:
  0.0 49.4 jit_solution(872076413227140235)
XLA Ops:
  0.0 48.0 %frame.1 = bf16[16,1024]{1,0:T(8,128)(2,1)} custom-call(bf16[256,512]{1,0:T(8,128)(2,1)} %x_hbm.1, bf16[16,1280]{1,0:T(8,128)(2,1)} %bitcast.15, bf16[16,2,1024,128]{3,2,1,0:T(8,128)(2,1)} %bitcast.9, s32[16]{0:T(128)} %lens_hbm.1, bf16[1024,512]{1,0:T(8,128)(2,1)} %wo_hbm.1, f32[1,512]{1,0:T(1,128)} %bitcast.16, bf16[512,1024]{1,0:T(8,128)(2,1)} %bitcast.12, ...), custom_call_target="tpu_custom_call" | custom-call | flops 1000000000 | bytes 19000000 | tf_op jit(solution)/shard_map/frame/pallas_call | solution.py:475
  48.0 1.4 %copy.14 = bf16[16,1,1024]{2,0,1:T(8,128)(2,1)} copy(bf16[16,1,1024]{2,0,1:T(8,128)(2,1)} %bitcast.14) | data formatting | bytes 65536

commit v3 on v2

--- a/solution.py
+++ b/solution.py
@@ -83,24 +83,8 @@
     d_in,
     e_out,
     e_in,
-    a_send,
-    a_recv,
-    f_send,
-    f_recv,
-    b_send,
-    b_recv,
-    h_send,
-    h_recv,
-    c_send,
-    c_recv,
-    d_send,
-    d_recv,
-    e_send,
-    e_recv,
-    l_send,
-    l_recv,
-    sib_send,
-    sib_recv,
+    direct_sem,
+    sems,
 ):
     s = lax.axis_index("sess")
     t = lax.axis_index("tp")
@@ -112,7 +96,7 @@
     sibling = (chip * 2 + other, t)
 
     def step_of(d):
-        return ((0, 1), (0, 3), (1, 0), (0, 2), (1, 1), (1, 3), (1, 2))[d - 1]
+        return ((0, 0), (0, 1), (0, 3), (1, 0), (0, 2), (1, 1), (1, 3), (1, 2))[d]
 
     def at(i, d):
         hi, lo = step_of(d)
@@ -134,6 +118,9 @@
             device_id=device,
             device_id_type=MESH,
         )
+
+    def settle(ref, sem):
+        pltpu.make_async_copy(ref, ref, sem).wait()
 
     def load(i, src, dst):
         return pltpu.make_async_copy(src, dst, in_sem.at[i])
@@ -212,7 +199,7 @@
     wo_load.start()
     win_load.start()
     pl.semaphore_wait(barrier, 22)
-    look_to_sib = remote(look_sib, look_in_sib, sib_send.at[0], sib_recv.at[0], sibling)
+    look_to_sib = remote(look_sib, look_in_sib, sems.at[0], sems.at[1], sibling)
     look_to_sib.start()
 
     frame = lax.broadcasted_iota(jnp.int32, (FRAMES, HD), 0)
@@ -237,12 +224,11 @@
     mine = attn_all.at[chip, core]
     gather = {}
     for d in far_first:
-        gather[d] = remote(mine, mine, a_send.at[d], a_recv.at[d], (at(chip, d) * 2 + other, t))
+        gather[d] = remote(mine, mine, sems.at[2], direct_sem.at[d - 1], (at(chip, d) * 2 + other, t))
         gather[d].start()
         if d == 7:
-            far = remote(mine, mine, f_send.at[d], f_recv.at[d], (at(chip, d) * 2 + core, t))
-            far.start()
-    swap = remote(mine, mine, f_send.at[0], f_recv.at[0], sibling)
+            remote(mine, mine, sems.at[3], sems.at[4], (at(chip, d) * 2 + core, t)).start()
+    swap = remote(mine, mine, sems.at[5], sems.at[6], sibling)
     swap.start()
 
     gain_load.wait()
@@ -251,96 +237,80 @@
     for j in range(DDEP // 128):
         cols = slice(j * 128, (j + 1) * 128)
         win[:, cols] = (win[:, cols].astype(F32) * gain_col).astype(BF16)
-    look_to_sib.wait()
+    look_to_sib.wait_recv()
     look_out[...] = (look_own[...].astype(F32) + look_in_sib[...].astype(F32)).astype(BF16)
 
-    across = [far]
     for d in near_first:
         gather[d].wait_recv()
         if d < 7:
             block = attn_all.at[back(chip, d), other]
-            copy = remote(block, block, f_send.at[d], f_recv.at[d], sibling)
-            copy.start()
-            across.append(copy)
+            remote(block, block, sems.at[3], sems.at[4], sibling).start()
     swap.wait_recv()
     wo_load.wait()
-
-    reduce_tp = [{}, {}]
 
     def reduce_start(half, parity):
         rows = attn_all[:, pl.ds(parity, 1)].reshape(CHIPS * ROWS, GROUP * HD)
         part[half] = dot(rows, wo[...]).astype(BF16).reshape(CHIPS, ROWS, COLS)
         for d in far_first:
             to = at(t, d)
-            copy = remote(part.at[half, to], part_in.at[half, d], b_send.at[half, d], b_recv.at[half, d], (s, to))
-            copy.start()
-            reduce_tp[half][d] = copy
+            remote(part.at[half, to], part_in.at[half, d - 1], sems.at[7 + half], sems.at[9 + half], (s, to)).start()
 
     reduce_start(0, other)
-    for copy in across:
-        copy.wait_recv()
+    settle(look_in, sems.at[4])
     reduce_start(1, core)
-    look_copies = []
     for d in far_first:
         to = at(chip, d)
-        copy = remote(look_out.at[to], look_in.at[d], l_send.at[d], l_recv.at[d], (to * 2 + core, t))
-        copy.start()
-        look_copies.append(copy)
+        remote(look_out.at[to], look_in.at[d - 1], sems.at[15], sems.at[16], (to * 2 + core, t)).start()
     x_load.wait()
-    gather_tp = [[], []]
 
     def gather_start(half, parity):
         hidden = xres[pl.ds(pl.multiple_of(parity * ROWS, ROWS), ROWS)].astype(F32) + part[half, t].astype(F32)
-        for d in near_first:
-            reduce_tp[half][d].wait_recv()
+        settle(part_in.at[half], sems.at[9 + half])
+        for d in range(CHIPS - 1):
             hidden = hidden + part_in[half, d].astype(F32)
         hid_all[t, parity] = hidden.astype(BF16)
         block = hid_all.at[t, parity]
         for d in far_first:
-            copy = remote(block, block, h_send.at[half, d], h_recv.at[half, d], (s, at(t, d)))
-            copy.start()
-            gather_tp[half].append(copy)
+            remote(block, block, sems.at[11 + half], sems.at[13 + half], (s, at(t, d))).start()
 
     gather_start(0, other)
     gather_start(1, core)
 
-    lane = lax.broadcasted_iota(jnp.int32, (CHIPS * ROWS, 128), 1)
-
-    def project(parity):
-        rows = hid_all[:, pl.ds(parity, 1)].reshape(CHIPS * ROWS, COLS)
+    lane = lax.broadcasted_iota(jnp.int32, (4 * ROWS, 128), 1)
+
+    def project(parity, blocks):
+        rows = jnp.concatenate([hid_all[i, parity] for i in blocks], axis=0)
         wide = rows.astype(F32)
         squares = jnp.sum(wide * wide, axis=1, keepdims=True)
         high = squares.astype(BF16).astype(F32)
         low = squares - high
         extra = jnp.where(lane == 2 * core, high, 0.0) + jnp.where(lane == 2 * core + 1, low, 0.0)
-        return dot(rows, win[...]).reshape(CHIPS, ROWS, DDEP), extra.reshape(CHIPS, ROWS, 128)
-
-    for copy in gather_tp[0]:
-        copy.wait_recv()
-    product, extra = project(other)
-    c_sib[:, :, :DDEP] = product.astype(BF16)
-    c_sib[:, :, DDEP:] = extra.astype(BF16)
-    to_sib = remote(c_sib, c_in_sib, sib_send.at[1], sib_recv.at[1], sibling)
+        return dot(rows, win[...]).reshape(len(blocks), ROWS, DDEP), extra.reshape(len(blocks), ROWS, 128)
+
+    settle(part_in.at[0], sems.at[13])
+    for blocks in (range(4), range(4, 8)):
+        product, extra = project(other, blocks)
+        c_sib[blocks[0] : blocks[0] + 4, :, :DDEP] = product.astype(BF16)
+        c_sib[blocks[0] : blocks[0] + 4, :, DDEP:] = extra.astype(BF16)
+    to_sib = remote(c_sib, c_in_sib, sems.at[17], sems.at[18], sibling)
     to_sib.start()
+    settle(look_in, sems.at[16])
     looked = look_out[chip].astype(F32)
-    for d in range(1, CHIPS):
-        look_copies[7 - d].wait_recv()
+    for d in range(CHIPS - 1):
         looked = looked + look_in[d].astype(F32)
-    for copy in gather_tp[1]:
-        copy.wait_recv()
-    to_sib.wait()
-    product, extra = project(core)
-    c_out[:, :, :DDEP] = (product + c_in_sib[:, :, :DDEP].astype(F32)).astype(BF16)
-    c_out[:, :, DDEP:] = (extra + c_in_sib[:, :, DDEP:].astype(F32)).astype(BF16)
-    reduce_sess = {}
-    for d in far_first:
-        to = at(chip, d)
-        copy = remote(c_out.at[to], c_in.at[d], c_send.at[d], c_recv.at[d], (to * 2 + core, t))
-        copy.start()
-        reduce_sess[d] = copy
-    summed = c_out[chip].astype(F32)
-    for d in near_first:
-        reduce_sess[d].wait_recv()
+    settle(part_in.at[1], sems.at[14])
+    to_sib.wait_recv()
+    for offsets in ((7, 6, 5, 4), (3, 2, 1, 0)):
+        product, extra = project(core, [at(chip, d) for d in offsets])
+        for i, d in enumerate(offsets):
+            to = at(chip, d)
+            c_out[d, :, :DDEP] = (product[i] + c_in_sib[to, :, :DDEP].astype(F32)).astype(BF16)
+            c_out[d, :, DDEP:] = (extra[i] + c_in_sib[to, :, DDEP:].astype(F32)).astype(BF16)
+            if d:
+                remote(c_out.at[d], c_in.at[d - 1], sems.at[19], sems.at[20], (to * 2 + core, t)).start()
+    summed = c_out[0].astype(F32)
+    settle(c_in, sems.at[20])
+    for d in range(CHIPS - 1):
         summed = summed + c_in[d].astype(F32)
     squares = jnp.sum(summed[:, DDEP:], axis=1, keepdims=True)
     depth_in = summed[:, :DDEP] * lax.rsqrt(squares / D + EPS) + looked
@@ -349,32 +319,22 @@
     mean_sq = jnp.mean(depth_in * depth_in, axis=1, keepdims=True)
     normed = (depth_in * lax.rsqrt(mean_sq + EPS) * dgain[...]).astype(BF16)
     dqkv_load.wait()
-    for u in range(4):
-        for p in range(3):
-            first = p * DDEP + u * QUAD
-            d_out[u, :, p * QUAD : (p + 1) * QUAD] = dot(normed, dqkv[:, first : first + QUAD]).astype(BF16)
-    down = []
     for e in (2, 1, 3, 0):
         to = (col + e) % 4
-        source = d_out.at[to, :, QUAD:]
-        down.append(
-            remote(source, d_in.at[t, :, QUAD:], d_send.at[4 + e], d_recv.at[4 + e], (s, 4 + to))
-        )
-
-    @pl.when(row == 0)
-    def _():
-        for copy in down:
-            copy.start()
-
-    heads_out = []
-    for e in (2, 1, 3):
-        to = (col + e) % 4
-        copy = remote(d_out.at[to], d_in.at[t], d_send.at[e], d_recv.at[e], (s, row * 4 + to))
-        copy.start()
-        heads_out.append(copy)
-    d_in[t] = d_out[col]
-    for copy in heads_out:
-        copy.wait_recv()
+        for p in range(3):
+            first = pl.multiple_of(p * DDEP + to * QUAD, QUAD)
+            d_out[e, :, p * QUAD : (p + 1) * QUAD] = dot(normed, dqkv[:, pl.ds(first, QUAD)]).astype(BF16)
+
+        @pl.when(row == 0)
+        def _(e=e, to=to):
+            remote(
+                d_out.at[e, :, QUAD:], d_in.at[t, :, QUAD:], sems.at[21], sems.at[22], (s, 4 + to)
+            ).start()
+
+        if e:
+            remote(d_out.at[e], d_in.at[t], sems.at[23], sems.at[24], (s, row * 4 + to)).start()
+    d_in[t] = d_out[0]
+    settle(d_in.at[pl.ds(0, 3)], sems.at[24])
 
     head_r = lax.broadcasted_iota(jnp.int32, (QUAD, QUAD), 0) // DH
     head_c = lax.broadcasted_iota(jnp.int32, (QUAD, QUAD), 1) // DH
@@ -412,33 +372,38 @@
 
     @pl.when(row == 1)
     def _():
-        for copy in down:
-            copy.wait_recv()
+        settle(d_in.at[pl.ds(0, 4), :, QUAD:], sems.at[22])
         attend((4, 5, 6, 7))
 
-    heads_back = []
     for e in (2, 1, 3):
         to = (col + e) % 4
-        copy = remote(e_out.at[to], e_in.at[col], e_send.at[e], e_recv.at[e], (s, row * 4 + to))
-        copy.start()
-        heads_back.append(copy)
+        remote(e_out.at[to], e_in.at[col], sems.at[25], sems.at[26], (s, row * 4 + to)).start()
     e_in[col] = e_out[col]
     dout_load.wait()
-    for copy in heads_back:
-        copy.wait_recv()
+    settle(e_in.at[pl.ds(0, 3)], sems.at[26])
     context = jnp.concatenate([e_in[i] for i in range(4)], axis=1)
     out_ref[...] = (depth_in + dot(context, dout[...])).astype(BF16)
 
-    sent = list(gather.values()) + across + [swap] + gather_tp[0] + gather_tp[1] + look_copies + heads_out + heads_back
-    for copies in (reduce_tp[0], reduce_tp[1], reduce_sess):
-        sent += list(copies.values())
-    for copy in sent:
-        copy.wait_send()
+    for ref, i in (
+        (look_sib, 0),
+        (look_in, 2),
+        (look_in, 3),
+        (mine, 5),
+        (part_in.at[0], 7),
+        (part_in.at[1], 8),
+        (part_in.at[0], 11),
+        (part_in.at[1], 12),
+        (look_in, 15),
+        (c_sib, 17),
+        (c_in, 19),
+        (d_in.at[pl.ds(0, 3)], 23),
+        (e_in.at[pl.ds(0, 3)], 25),
+    ):
+        settle(ref, sems.at[i])
 
     @pl.when(row == 0)
     def _():
-        for copy in down:
-            copy.wait_send()
+        settle(d_in.at[pl.ds(0, 4), :, QUAD:], sems.at[21])
 
 
 def shards(
@@ -503,43 +468,27 @@
             vm((ROWS * GROUP, HD), F32),
             vm((CHIPS, 2, ROWS, GROUP * HD), BF16),
             vm((2, TP, ROWS, COLS), BF16),
-            vm((2, TP, ROWS, COLS), BF16),
+            vm((2, TP - 1, ROWS, COLS), BF16),
             vm((TP, 2, ROWS, COLS), BF16),
             vm((CHIPS, 2, ROWS, 128), BF16),
             vm((CHIPS, ROWS, DDEP), BF16),
             vm((CHIPS, ROWS, DDEP), BF16),
             vm((CHIPS, ROWS, DDEP), BF16),
             vm((CHIPS, ROWS, DDEP), BF16),
-            vm((CHIPS, ROWS, DDEP), BF16),
+            vm((CHIPS - 1, ROWS, DDEP), BF16),
             vm((CHIPS, ROWS, WIDE), BF16),
             vm((CHIPS, ROWS, WIDE), BF16),
             vm((CHIPS, ROWS, WIDE), BF16),
-            vm((CHIPS, ROWS, WIDE), BF16),
+            vm((CHIPS - 1, ROWS, WIDE), BF16),
             vm((4, ROWS, 3 * QUAD), BF16),
             vm((TP, ROWS, 3 * QUAD), BF16),
             vm((4, ROWS, QUAD), BF16),
             vm((4, ROWS, QUAD), BF16),
-            dma((8,)),
-            dma((8,)),
-            dma((8,)),
-            dma((8,)),
-            dma((2, 8)),
-            dma((2, 8)),
-            dma((2, 8)),
-            dma((2, 8)),
-            dma((8,)),
-            dma((8,)),
-            dma((8,)),
-            dma((8,)),
-            dma((4,)),
-            dma((4,)),
-            dma((8,)),
-            dma((8,)),
-            dma((2,)),
-            dma((2,)),
+            dma((7,)),
+            dma((27,)),
         ],
         compiler_params=pltpu.CompilerParams(
-            collective_id=0, has_side_effects=True, vmem_limit_bytes=62 * 2**20
+            collective_id=0, has_side_effects=True, vmem_limit_bytes=40 * 2**20
         ),
         cost_estimate=pl.CostEstimate(flops=10**9, bytes_accessed=19 * 10**6, transcendentals=10**5),
     )(*args)

time: 49.5 us -> 46.7 us (0.943)
  Pallas kernels: 48 us -> 46 us
  local copies, waits for them, and re-layouts: 1.38 us -> 0.62 us
    pallas_call x1, Pallas kernels: 48 us -> 46 us  [shards(): pl.pallas_call(frame_kernel, name='frame', out_shape=jax.ShapeDtypeStruct...]
    unnamed x1, local copies, waits for them, and re-layouts: 1.38 us -> 0.62 us
where the time goes in v3:
time: 46.7 us; the launch traced here: 46.6 us
  Pallas kernels  46 us (99%)
  local copies, waits for them, and re-layouts  0.62 us (1%)
    pallas_call x1, Pallas kernels, shards(): pl.pallas_call(frame_kernel, name='frame', out_shape=jax.ShapeDtypeStruct...  46 us

profile of v3, /device:TPU:0, one launch (start us, length us, event | category | flops | bytes accessed | tf_op | source)
XLA Modules:
  0.0 46.6 jit_solution(17211722224812801406)
XLA Ops:
  0.0 46.0 %frame.1 = bf16[16,1024]{1,0:T(8,128)(2,1)S(1)} custom-call(bf16[256,512]{1,0:T(8,128)(2,1)} %x_hbm.1, bf16[16,1280]{1,0:T(8,128)(2,1)} %bitcast.15, bf16[16,2,1024,128]{3,2,1,0:T(8,128)(2,1)} %bitcast.10, s32[16]{0:T(128)} %lens_hbm.1, bf16[1024,512]{1,0:T(8,128)(2,1)} %wo_hbm.1, f32[1,512]{1,0:T(1,128)} %bitcast.16, bf16[512,1024]{1,0:T(8,128)(2,1)} %bitcast.13, ...), custom_call_target="tpu_custom_call" | custom-call | flops 1000000000 | bytes 19000000 | tf_op jit(solution)/shard_map/frame/pallas_call | solution.py:440
  46.0 0.6 %copy.14 = bf16[16,1,1024]{2,0,1:T(8,128)(2,1)} copy(bf16[16,1,1024]{2,0,1:T(8,128)(2,1)S(1)} %bitcast.9) | data formatting | bytes 65536

commit v4 on v3

--- a/solution.py
+++ b/solution.py
@@ -22,7 +22,8 @@
 WIDE = DDEP + 128
 QUAD = 256
 DH = 64
-STEP = 4
+HALF = 8
+HALF_FRAMES = FRAMES // 2
 
 
 def dot(a, b):
@@ -62,7 +63,6 @@
     k_scr,
     v_scr,
     query_cols,
-    score_scr,
     weight_scr,
     o_scr,
     attn_all,
@@ -136,24 +136,23 @@
     win_load = load(8, win_hbm, win)
     dqkv_load = load(9, dqkv_hbm, dqkv)
     dout_load = load(10, dout_hbm, dout)
-    key_loads = [
-        pltpu.make_async_copy(kv_hbm.at[pl.ds(g * STEP, STEP), 0], keys.at[pl.ds(g * STEP, STEP)], kv_sem.at[0, g])
-        for g in range(ROWS // STEP)
-    ]
-    value_loads = [
-        pltpu.make_async_copy(kv_hbm.at[pl.ds(g * STEP, STEP), 1], values.at[pl.ds(g * STEP, STEP)], kv_sem.at[1, g])
-        for g in range(ROWS // STEP)
-    ]
-    for copy in [qkv_load, lens_load, tok_load, emb_load] + key_loads + value_loads:
-        copy.start()
-    for copy in (gain_load, dgain_load, x_load):
+    def cache_load(which, first, count, dst, i):
+        part_of = pl.ds(first, count)
+        return pltpu.make_async_copy(kv_hbm.at[part_of, which], dst.at[part_of], kv_sem.at[i])
+
+    key_loads = [cache_load(0, a * HALF, HALF, keys, a) for a in range(2)]
+    value_loads = [cache_load(1, g * 4, 4, values, 2 + g) for g in range(4)]
+    loads = [qkv_load, key_loads[0], lens_load, value_loads[0], value_loads[1], key_loads[1], value_loads[2], value_loads[3]]
+    for copy in loads:
         copy.start()
 
     barrier = pltpu.get_barrier_semaphore()
     pl.semaphore_signal(barrier, inc=1, device_id=sibling, device_id_type=MESH)
-    for d in near_first:
+    for d in far_first:
         for device in ((at(chip, d) * 2, t), (at(chip, d) * 2 + 1, t), (s, at(t, d))):
             pl.semaphore_signal(barrier, inc=1, device_id=device, device_id_type=MESH)
+    for copy in (tok_load, emb_load, gain_load, dgain_load, x_load):
+        copy.start()
 
     qkv_load.wait()
     new_keys = qkv[:, GROUP * HD : (GROUP + 1) * HD].astype(F32)
@@ -166,14 +165,90 @@
     query_t = q_scr[...].T
     scale = HD ** (-0.5)
     new_score = jnp.sum(query_t * k_scr[...].T, axis=0, keepdims=True) * scale
-    owner = lax.broadcasted_iota(jnp.int32, (HD, HD), 1) // GROUP
-    for i in range(ROWS):
-        query_cols[i * HD : (i + 1) * HD, :] = jnp.where(owner == i, query_t, 0.0).astype(BF16)
+    new_score = jnp.broadcast_to(new_score, (8, HD))
+    column = lax.broadcasted_iota(jnp.int32, (HD, HD), 1)
+    line = lax.broadcasted_iota(jnp.int32, (8, HD), 1)
+    swapped = pltpu.roll(query_t, 64, 1)
+    swapped_score = pltpu.roll(new_score, 64, 1)
     lens_load.wait()
-    owner_row = lax.broadcasted_iota(jnp.int32, (1, HD), 1) // GROUP
-    live = jnp.zeros((1, HD), jnp.int32)
-    for i in range(ROWS):
-        live = jnp.where(owner_row == i, lens[i], live)
+    half_scores = []
+    lives = []
+    for a in range(2):
+        half_query = jnp.where((column < 64) == (a == 0), query_t, swapped)
+        half_scores.append(jnp.where((line < 64) == (a == 0), new_score, swapped_score))
+        live = jnp.zeros((8, HD), jnp.int32)
+        for i in range(HALF):
+            live = jnp.where((line // GROUP) % HALF == i, lens[a * HALF + i], live)
+            for f in range(2):
+                block = f * HALF + i
+                query_cols[a, block * HD : (block + 1) * HD, :] = jnp.where(
+                    column // GROUP == block, half_query, 0.0
+                ).astype(BF16)
+        lives.append(live - jnp.where(line < 64, 0, HALF_FRAMES))
+    frame = lax.broadcasted_iota(jnp.int32, (HALF_FRAMES, HD), 0)
+
+    def attend_half(a):
+        key_loads[a].wait()
+        joined = jnp.concatenate(
+            [
+                keys[a * HALF + i, f * HALF_FRAMES : (f + 1) * HALF_FRAMES]
+                for f in range(2)
+                for i in range(HALF)
+            ],
+            axis=1,
+        )
+        scores = dot(joined, query_cols[a]) * scale
+        masked = jnp.where(frame < lives[a][:1], scores, -1e30)
+        top = jnp.broadcast_to(jnp.max(masked, axis=0, keepdims=True), (8, HD))
+        peak = jnp.maximum(jnp.maximum(top, pltpu.roll(top, 64, 1)), half_scores[a])
+        expo = jnp.exp(masked - peak[:1])
+        new_expo = jnp.exp(half_scores[a] - peak)
+        total = jnp.broadcast_to(jnp.sum(expo, axis=0, keepdims=True), (8, HD))
+        inv = 1.0 / (total + pltpu.roll(total, 64, 1) + new_expo)
+        weight_scr[...] = (expo * inv[:1]).T
+        new_weight = (new_expo * inv).astype(BF16).astype(F32)
+        new_column = jnp.broadcast_to(new_weight[:1], (HD, HD)).T
+        for g in range(2):
+            value_loads[a * 2 + g].wait()
+            for i in range(g * 4, g * 4 + 4):
+                session = a * HALF + i
+                rows_i = slice(i * GROUP, (i + 1) * GROUP)
+                rows_s = slice(session * GROUP, (session + 1) * GROUP)
+                context = new_column[rows_i] * v_scr[rows_s, :]
+                for f in range(2):
+                    weights = weight_scr[f * 64 + i * GROUP : f * 64 + (i + 1) * GROUP, :].astype(BF16)
+                    context = context + dot(weights, values[session, f * HALF_FRAMES : (f + 1) * HALF_FRAMES])
+                o_scr[rows_s, :] = context
+
+    gather = {}
+
+    def gather_half(a):
+        for h in range(4):
+            low_heads = o_scr[pl.ds(a * 64 + h, HALF, stride=GROUP), :]
+            high_heads = o_scr[pl.ds(a * 64 + h + 4, HALF, stride=GROUP), :]
+            attn_all[a, chip, core, :, h * HD : (h + 1) * HD] = jnp.concatenate(
+                [low_heads, high_heads], axis=0
+            ).astype(BF16)
+        mine = attn_all.at[a, chip, core]
+        if a == 0:
+            pl.semaphore_wait(barrier, 22)
+        for d in far_first:
+            gather[a, d] = remote(
+                mine, mine, sems.at[2], direct_sem.at[a * 7 + d - 1], (at(chip, d) * 2 + other, t)
+            )
+            gather[a, d].start()
+            if d == 7:
+                remote(mine, mine, sems.at[3], sems.at[4], (at(chip, d) * 2 + core, t)).start()
+        remote(mine, mine, sems.at[5], sems.at[6], sibling).start()
+
+    attend_half(0)
+    gather_half(0)
+    wo_load.start()
+    win_load.start()
+    attend_half(1)
+    gather_half(1)
+    dqkv_load.start()
+    dout_load.start()
 
     tok_load.wait()
     emb_load.wait()
@@ -186,50 +261,9 @@
         return dot(rows, emb[...]).astype(BF16).reshape(CHIPS, ROWS, DDEP)
 
     look_sib[...] = look(other)
-    look_own[...] = look(core)
-
-    for g in range(ROWS // STEP):
-        key_loads[g].wait()
-        joined = jnp.concatenate([keys[g * STEP + i] for i in range(STEP)], axis=1)
-        scores = dot(joined, query_cols[g * STEP * HD : (g + 1) * STEP * HD, :])
-        if g == 0:
-            score_scr[...] = scores
-        else:
-            score_scr[...] += scores
-    wo_load.start()
-    win_load.start()
-    pl.semaphore_wait(barrier, 22)
     look_to_sib = remote(look_sib, look_in_sib, sems.at[0], sems.at[1], sibling)
     look_to_sib.start()
-
-    frame = lax.broadcasted_iota(jnp.int32, (FRAMES, HD), 0)
-    masked = jnp.where(frame < live, score_scr[...] * scale, -1e30)
-    peak = jnp.maximum(jnp.max(masked, axis=0, keepdims=True), new_score)
-    expo = jnp.exp(masked - peak)
-    new_expo = jnp.exp(new_score - peak)
-    inv = 1.0 / (jnp.sum(expo, axis=0, keepdims=True) + new_expo)
-    weight_scr[...] = (expo * inv).T
-    new_weight = (new_expo * inv).astype(BF16).astype(F32)
-    o_scr[...] = jnp.broadcast_to(new_weight, (HD, HD)).T * v_scr[...]
-    for g in range(ROWS // STEP):
-        value_loads[g].wait()
-        for i in range(g * STEP, (g + 1) * STEP):
-            rows_i = slice(i * GROUP, (i + 1) * GROUP)
-            o_scr[rows_i, :] += dot(weight_scr[rows_i, :].astype(BF16), values[i])
-    dqkv_load.start()
-    dout_load.start()
-
-    for h in range(GROUP):
-        attn_all[chip, core, :, h * HD : (h + 1) * HD] = o_scr[pl.ds(h, ROWS, stride=GROUP), :].astype(BF16)
-    mine = attn_all.at[chip, core]
-    gather = {}
-    for d in far_first:
-        gather[d] = remote(mine, mine, sems.at[2], direct_sem.at[d - 1], (at(chip, d) * 2 + other, t))
-        gather[d].start()
-        if d == 7:
-            remote(mine, mine, sems.at[3], sems.at[4], (at(chip, d) * 2 + core, t)).start()
-    swap = remote(mine, mine, sems.at[5], sems.at[6], sibling)
-    swap.start()
+    look_own[...] = look(core)
 
     gain_load.wait()
     win_load.wait()
@@ -237,20 +271,26 @@
     for j in range(DDEP // 128):
         cols = slice(j * 128, (j + 1) * 128)
         win[:, cols] = (win[:, cols].astype(F32) * gain_col).astype(BF16)
-    look_to_sib.wait_recv()
-    look_out[...] = (look_own[...].astype(F32) + look_in_sib[...].astype(F32)).astype(BF16)
-
-    for d in near_first:
-        gather[d].wait_recv()
-        if d < 7:
-            block = attn_all.at[back(chip, d), other]
-            remote(block, block, sems.at[3], sems.at[4], sibling).start()
-    swap.wait_recv()
+
+    for a in range(2):
+        for d in near_first:
+            gather[a, d].wait_recv()
+            if d < 7:
+                block = attn_all.at[a, back(chip, d), other]
+                remote(block, block, sems.at[3], sems.at[4], sibling).start()
+    settle(look_in.at[0], sems.at[6])
     wo_load.wait()
 
+    def attention_rows(parity):
+        blocks = []
+        for i in range(CHIPS):
+            for a in range(2):
+                block = attn_all[a, i, parity].astype(F32)
+                blocks.append(jnp.concatenate([block[:HALF], block[HALF:]], axis=1))
+        return jnp.concatenate(blocks, axis=0).astype(BF16)
+
     def reduce_start(half, parity):
-        rows = attn_all[:, pl.ds(parity, 1)].reshape(CHIPS * ROWS, GROUP * HD)
-        part[half] = dot(rows, wo[...]).astype(BF16).reshape(CHIPS, ROWS, COLS)
+        part[half] = dot(attention_rows(parity), wo[...]).astype(BF16).reshape(CHIPS, ROWS, COLS)
         for d in far_first:
             to = at(t, d)
             remote(part.at[half, to], part_in.at[half, d - 1], sems.at[7 + half], sems.at[9 + half], (s, to)).start()
@@ -258,6 +298,8 @@
     reduce_start(0, other)
     settle(look_in, sems.at[4])
     reduce_start(1, core)
+    look_to_sib.wait_recv()
+    look_out[...] = (look_own[...].astype(F32) + look_in_sib[...].astype(F32)).astype(BF16)
     for d in far_first:
         to = at(chip, d)
         remote(look_out.at[to], look_in.at[d - 1], sems.at[15], sems.at[16], (to * 2 + core, t)).start()
@@ -288,26 +330,31 @@
         return dot(rows, win[...]).reshape(len(blocks), ROWS, DDEP), extra.reshape(len(blocks), ROWS, 128)
 
     settle(part_in.at[0], sems.at[13])
-    for blocks in (range(4), range(4, 8)):
-        product, extra = project(other, blocks)
-        c_sib[blocks[0] : blocks[0] + 4, :, :DDEP] = product.astype(BF16)
-        c_sib[blocks[0] : blocks[0] + 4, :, DDEP:] = extra.astype(BF16)
-    to_sib = remote(c_sib, c_in_sib, sems.at[17], sems.at[18], sibling)
-    to_sib.start()
+    to_sib = {}
+    for k, offsets in enumerate(((7, 6, 5, 4), (3, 2, 1, 0))):
+        product, extra = project(other, [at(chip, d) for d in offsets])
+        for i, d in enumerate(offsets):
+            c_sib[d, :, :DDEP] = product[i].astype(BF16)
+            c_sib[d, :, DDEP:] = extra[i].astype(BF16)
+        part_of = pl.ds(offsets[3], 4)
+        to_sib[k] = remote(
+            c_sib.at[part_of], c_in_sib.at[part_of], sems.at[17], sems.at[18 if k == 0 else 27], sibling
+        )
+        to_sib[k].start()
+    settle(part_in.at[1], sems.at[14])
+    for k, offsets in enumerate(((7, 6, 5, 4), (3, 2, 1, 0))):
+        product, extra = project(core, [at(chip, d) for d in offsets])
+        to_sib[k].wait_recv()
+        for i, d in enumerate(offsets):
+            to = at(chip, d)
+            c_out[d, :, :DDEP] = (product[i] + c_in_sib[d, :, :DDEP].astype(F32)).astype(BF16)
+            c_out[d, :, DDEP:] = (extra[i] + c_in_sib[d, :, DDEP:].astype(F32)).astype(BF16)
+            if d:
+                remote(c_out.at[d], c_in.at[d - 1], sems.at[19], sems.at[20], (to * 2 + core, t)).start()
     settle(look_in, sems.at[16])
     looked = look_out[chip].astype(F32)
     for d in range(CHIPS - 1):
         looked = looked + look_in[d].astype(F32)
-    settle(part_in.at[1], sems.at[14])
-    to_sib.wait_recv()
-    for offsets in ((7, 6, 5, 4), (3, 2, 1, 0)):
-        product, extra = project(core, [at(chip, d) for d in offsets])
-        for i, d in enumerate(offsets):
-            to = at(chip, d)
-            c_out[d, :, :DDEP] = (product[i] + c_in_sib[to, :, :DDEP].astype(F32)).astype(BF16)
-            c_out[d, :, DDEP:] = (extra[i] + c_in_sib[to, :, DDEP:].astype(F32)).astype(BF16)
-            if d:
-                remote(c_out.at[d], c_in.at[d - 1], sems.at[19], sems.at[20], (to * 2 + core, t)).start()
     summed = c_out[0].astype(F32)
     settle(c_in, sems.at[20])
     for d in range(CHIPS - 1):
@@ -388,7 +435,7 @@
         (look_sib, 0),
         (look_in, 2),
         (look_in, 3),
-        (mine, 5),
+        (look_in.at[0], 5),
         (part_in.at[0], 7),
         (part_in.at[1], 8),
         (part_in.at[0], 11),
@@ -457,16 +504,15 @@
             vm((1, COLS), F32),
             vm((1, DDEP), F32),
             vm((1, 256), jnp.int32),
-            dma((2, ROWS // STEP)),
+            dma((6,)),
             dma((11,)),
             vm((ROWS * GROUP, HD), F32),
             vm((ROWS * GROUP, HD), F32),
             vm((ROWS * GROUP, HD), F32),
-            vm((ROWS * HD, HD), BF16),
-            vm((FRAMES, HD), F32),
-            vm((ROWS * GROUP, FRAMES), F32),
+            vm((2, ROWS * HD, HD), BF16),
+            vm((HD, HALF_FRAMES), F32),
             vm((ROWS * GROUP, HD), F32),
-            vm((CHIPS, 2, ROWS, GROUP * HD), BF16),
+            vm((2, CHIPS, 2, ROWS, GROUP * HD // 2), BF16),
             vm((2, TP, ROWS, COLS), BF16),
             vm((2, TP - 1, ROWS, COLS), BF16),
             vm((TP, 2, ROWS, COLS), BF16),
@@ -484,8 +530,8 @@
             vm((TP, ROWS, 3 * QUAD), BF16),
             vm((4, ROWS, QUAD), BF16),
             vm((4, ROWS, QUAD), BF16),
-            dma((7,)),
-            dma((27,)),
+            dma((14,)),
+            dma((28,)),
         ],
         compiler_params=pltpu.CompilerParams(
             collective_id=0, has_side_effects=True, vmem_limit_bytes=40 * 2**20

time: 46.7 us -> 45.1 us (0.966)
  Pallas kernels: 46 us -> 44.4 us
    pallas_call x1, Pallas kernels: 46 us -> 44.4 us  [shards(): pl.pallas_call(frame_kernel, name='frame', out_shape=jax.ShapeDtypeStruct...]
where the time goes in v4:
time: 45.1 us; the launch traced here: 45 us
  Pallas kernels  44.4 us (98%)
  local copies, waits for them, and re-layouts  0.62 us (1%)
    pallas_call x1, Pallas kernels, shards(): pl.pallas_call(frame_kernel, name='frame', out_shape=jax.ShapeDtypeStruct...  44.4 us

profile of v4, /device:TPU:0, one launch (start us, length us, event | category | flops | bytes accessed | tf_op | source)
XLA Modules:
  0.0 45.0 jit_solution(7581022288672940583)
XLA Ops:
  0.0 44.4 %frame.1 = bf16[16,1024]{1,0:T(8,128)(2,1)S(1)} custom-call(bf16[256,512]{1,0:T(8,128)(2,1)} %x_hbm.1, bf16[16,1280]{1,0:T(8,128)(2,1)} %bitcast.15, bf16[16,2,1024,128]{3,2,1,0:T(8,128)(2,1)} %bitcast.10, s32[16]{0:T(128)} %lens_hbm.1, bf16[1024,512]{1,0:T(8,128)(2,1)} %wo_hbm.1, f32[1,512]{1,0:T(1,128)} %bitcast.16, bf16[512,1024]{1,0:T(8,128)(2,1)} %bitcast.13, ...), custom_call_target="tpu_custom_call" | custom-call | flops 1000000000 | bytes 19000000 | tf_op jit(solution)/shard_map/frame/pallas_call | solution.py:487
  44.4 0.6 %copy.14 = bf16[16,1,1024]{2,0,1:T(8,128)(2,1)} copy(bf16[16,1,1024]{2,0,1:T(8,128)(2,1)S(1)} %bitcast.9) | data formatting | bytes 65536

commit v5 on v4

--- a/solution.py
+++ b/solution.py
@@ -210,15 +210,19 @@
         new_column = jnp.broadcast_to(new_weight[:1], (HD, HD)).T
         for g in range(2):
             value_loads[a * 2 + g].wait()
-            for i in range(g * 4, g * 4 + 4):
+            for i in range(g * 4, g * 4 + 4, 2):
                 session = a * HALF + i
-                rows_i = slice(i * GROUP, (i + 1) * GROUP)
-                rows_s = slice(session * GROUP, (session + 1) * GROUP)
-                context = new_column[rows_i] * v_scr[rows_s, :]
+                context = None
                 for f in range(2):
-                    weights = weight_scr[f * 64 + i * GROUP : f * 64 + (i + 1) * GROUP, :].astype(BF16)
-                    context = context + dot(weights, values[session, f * HALF_FRAMES : (f + 1) * HALF_FRAMES])
-                o_scr[rows_s, :] = context
+                    rows_f = slice(f * 64 + i * GROUP, f * 64 + (i + 2) * GROUP)
+                    frames = slice(f * HALF_FRAMES, (f + 1) * HALF_FRAMES)
+                    pair = jnp.concatenate([values[session, frames], values[session + 1, frames]], axis=1)
+                    partial = dot(weight_scr[rows_f, :].astype(BF16), pair)
+                    context = partial if f == 0 else context + partial
+                rows_i = slice(i * GROUP, (i + 2) * GROUP)
+                rows_s = slice(session * GROUP, (session + 2) * GROUP)
+                own = jnp.concatenate([context[:GROUP, :HD], context[GROUP:, HD:]], axis=0)
+                o_scr[rows_s, :] = own + new_column[rows_i] * v_scr[rows_s, :]
 
     gather = {}
 
@@ -281,19 +285,24 @@
     settle(look_in.at[0], sems.at[6])
     wo_load.wait()
 
-    def attention_rows(parity):
+    def attention_rows(parity, chips):
         blocks = []
-        for i in range(CHIPS):
+        for i in chips:
             for a in range(2):
                 block = attn_all[a, i, parity].astype(F32)
                 blocks.append(jnp.concatenate([block[:HALF], block[HALF:]], axis=1))
         return jnp.concatenate(blocks, axis=0).astype(BF16)
 
     def reduce_start(half, parity):
-        part[half] = dot(attention_rows(parity), wo[...]).astype(BF16).reshape(CHIPS, ROWS, COLS)
-        for d in far_first:
-            to = at(t, d)
-            remote(part.at[half, to], part_in.at[half, d - 1], sems.at[7 + half], sems.at[9 + half], (s, to)).start()
+        for offsets in ((7, 6, 5, 4), (3, 2, 1, 0)):
+            rows = attention_rows(parity, [at(t, d) for d in offsets])
+            product = dot(rows, wo[...]).astype(BF16).reshape(4, ROWS, COLS)
+            for i, d in enumerate(offsets):
+                part[half, d] = product[i]
+                if d:
+                    remote(
+                        part.at[half, d], part_in.at[half, d - 1], sems.at[7 + half], sems.at[9 + half], (s, at(t, d))
+                    ).start()
 
     reduce_start(0, other)
     settle(look_in, sems.at[4])
@@ -306,7 +315,7 @@
     x_load.wait()
 
     def gather_start(half, parity):
-        hidden = xres[pl.ds(pl.multiple_of(parity * ROWS, ROWS), ROWS)].astype(F32) + part[half, t].astype(F32)
+        hidden = xres[pl.ds(pl.multiple_of(parity * ROWS, ROWS), ROWS)].astype(F32) + part[half, 0].astype(F32)
         settle(part_in.at[half], sems.at[9 + half])
         for d in range(CHIPS - 1):
             hidden = hidden + part_in[half, d].astype(F32)
@@ -422,14 +431,22 @@
         settle(d_in.at[pl.ds(0, 4), :, QUAD:], sems.at[22])
         attend((4, 5, 6, 7))
 
-    for e in (2, 1, 3):
+    back_copies = {}
+    for k, e in enumerate((2, 1, 3)):
         to = (col + e) % 4
-        remote(e_out.at[to], e_in.at[col], sems.at[25], sems.at[26], (s, row * 4 + to)).start()
-    e_in[col] = e_out[col]
+        back_copies[e] = remote(e_out.at[to], e_in.at[e], sems.at[25], sems.at[(26, 28, 29)[k]], (s, row * 4 + to))
+        back_copies[e].start()
+
+    def project_out(block, source):
+        first = pl.multiple_of(source * QUAD, QUAD)
+        return dot(block, dout[pl.ds(first, QUAD), :])
+
     dout_load.wait()
-    settle(e_in.at[pl.ds(0, 3)], sems.at[26])
-    context = jnp.concatenate([e_in[i] for i in range(4)], axis=1)
-    out_ref[...] = (depth_in + dot(context, dout[...])).astype(BF16)
+    result = depth_in + project_out(e_out[col], col)
+    for e in (1, 3, 2):
+        back_copies[e].wait_recv()
+        result = result + project_out(e_in[e], (col + 4 - e) % 4)
+    out_ref[...] = result.astype(BF16)
 
     for ref, i in (
         (look_sib, 0),
@@ -531,7 +548,7 @@
             vm((4, ROWS, QUAD), BF16),
             vm((4, ROWS, QUAD), BF16),
             dma((14,)),
-            dma((28,)),
+            dma((30,)),
         ],
         compiler_params=pltpu.CompilerParams(
             collective_id=0, has_side_effects=True, vmem_limit_bytes=40 * 2**20

time: 45.1 us -> 45.3 us (level)
  no operation moved by 1% of the time
where the time goes in v5:
time: 45.3 us; the launch traced here: 45.1 us
  Pallas kernels  44.5 us (98%)
  local copies, waits for them, and re-layouts  0.62 us (1%)
    pallas_call x1, Pallas kernels, shards(): pl.pallas_call(frame_kernel, name='frame', out_shape=jax.ShapeDtypeStruct...  44.5 us

profile of v5, /device:TPU:0, one launch (start us, length us, event | category | flops | bytes accessed | tf_op | source)
XLA Modules:
  0.0 45.1 jit_solution(1857330406412021610)
XLA Ops:
  0.0 44.5 %frame.1 = bf16[16,1024]{1,0:T(8,128)(2,1)S(1)} custom-call(bf16[256,512]{1,0:T(8,128)(2,1)} %x_hbm.1, bf16[16,1280]{1,0:T(8,128)(2,1)} %bitcast.15, bf16[16,2,1024,128]{3,2,1,0:T(8,128)(2,1)} %bitcast.10, s32[16]{0:T(128)} %lens_hbm.1, bf16[1024,512]{1,0:T(8,128)(2,1)} %wo_hbm.1, f32[1,512]{1,0:T(1,128)} %bitcast.16, bf16[512,1024]{1,0:T(8,128)(2,1)} %bitcast.13, ...), custom_call_target="tpu_custom_call" | custom-call | flops 1000000000 | bytes 19000000 | tf_op jit(solution)/shard_map/frame/pallas_call | solution.py:504
  44.5 0.6 %copy.14 = bf16[16,1,1024]{2,0,1:T(8,128)(2,1)} copy(bf16[16,1,1024]{2,0,1:T(8,128)(2,1)S(1)} %bitcast.9) | data formatting | bytes 65536

commit v6 on v5

--- a/solution.py
+++ b/solution.py
@@ -307,11 +307,6 @@
     reduce_start(0, other)
     settle(look_in, sems.at[4])
     reduce_start(1, core)
-    look_to_sib.wait_recv()
-    look_out[...] = (look_own[...].astype(F32) + look_in_sib[...].astype(F32)).astype(BF16)
-    for d in far_first:
-        to = at(chip, d)
-        remote(look_out.at[to], look_in.at[d - 1], sems.at[15], sems.at[16], (to * 2 + core, t)).start()
     x_load.wait()
 
     def gather_start(half, parity):
@@ -326,6 +321,11 @@
 
     gather_start(0, other)
     gather_start(1, core)
+    look_to_sib.wait_recv()
+    look_out[...] = (look_own[...].astype(F32) + look_in_sib[...].astype(F32)).astype(BF16)
+    for d in far_first:
+        to = at(chip, d)
+        remote(look_out.at[to], look_in.at[d - 1], sems.at[15], sems.at[16], (to * 2 + core, t)).start()
 
     lane = lax.broadcasted_iota(jnp.int32, (4 * ROWS, 128), 1)
 

time: 45.3 us -> 43.1 us (0.951)
  Pallas kernels: 44.5 us -> 42.3 us
    pallas_call x1, Pallas kernels: 44.5 us -> 42.3 us  [shards(): pl.pallas_call(frame_kernel, name='frame', out_shape=jax.ShapeDtypeStruct...]
where the time goes in v6:
time: 43.1 us; the launch traced here: 43 us
  Pallas kernels  42.3 us (98%)
  local copies, waits for them, and re-layouts  0.62 us (1%)
    pallas_call x1, Pallas kernels, shards(): pl.pallas_call(frame_kernel, name='frame', out_shape=jax.ShapeDtypeStruct...  42.3 us

profile of v6, /device:TPU:0, one launch (start us, length us, event | category | flops | bytes accessed | tf_op | source)
XLA Modules:
  0.0 43.0 jit_solution(10720304593733121747)
XLA Ops:
  0.0 42.3 %frame.1 = bf16[16,1024]{1,0:T(8,128)(2,1)S(1)} custom-call(bf16[256,512]{1,0:T(8,128)(2,1)} %x_hbm.1, bf16[16,1280]{1,0:T(8,128)(2,1)} %bitcast.15, bf16[16,2,1024,128]{3,2,1,0:T(8,128)(2,1)} %bitcast.10, s32[16]{0:T(128)} %lens_hbm.1, bf16[1024,512]{1,0:T(8,128)(2,1)} %wo_hbm.1, f32[1,512]{1,0:T(1,128)} %bitcast.16, bf16[512,1024]{1,0:T(8,128)(2,1)} %bitcast.13, ...), custom_call_target="tpu_custom_call" | custom-call | flops 1000000000 | bytes 19000000 | tf_op jit(solution)/shard_map/frame/pallas_call | solution.py:504
  42.3 0.6 %copy.14 = bf16[16,1,1024]{2,0,1:T(8,128)(2,1)} copy(bf16[16,1,1024]{2,0,1:T(8,128)(2,1)S(1)} %bitcast.9) | data formatting | bytes 65536

commit v7 on v6

--- a/solution.py
+++ b/solution.py
@@ -241,8 +241,6 @@
                 mine, mine, sems.at[2], direct_sem.at[a * 7 + d - 1], (at(chip, d) * 2 + other, t)
             )
             gather[a, d].start()
-            if d == 7:
-                remote(mine, mine, sems.at[3], sems.at[4], (at(chip, d) * 2 + core, t)).start()
         remote(mine, mine, sems.at[5], sems.at[6], sibling).start()
 
     attend_half(0)
@@ -279,9 +277,8 @@
     for a in range(2):
         for d in near_first:
             gather[a, d].wait_recv()
-            if d < 7:
-                block = attn_all.at[a, back(chip, d), other]
-                remote(block, block, sems.at[3], sems.at[4], sibling).start()
+            block = attn_all.at[a, back(chip, d), other]
+            remote(block, block, sems.at[3], sems.at[4], sibling).start()
     settle(look_in.at[0], sems.at[6])
     wo_load.wait()
 

time: 43.1 us -> 42.9 us (level)
  no operation moved by 1% of the time
where the time goes in v7:
time: 42.9 us; the launch traced here: 42.8 us
  Pallas kernels  42.2 us (98%)
  local copies, waits for them, and re-layouts  0.62 us (1%)
    pallas_call x1, Pallas kernels, shards(): pl.pallas_call(frame_kernel, name='frame', out_shape=jax.ShapeDtypeStruct...  42.2 us

profile of v7, /device:TPU:0, one launch (start us, length us, event | category | flops | bytes accessed | tf_op | source)
XLA Modules:
  0.0 42.8 jit_solution(1765372088857715470)
XLA Ops:
  0.0 42.2 %frame.1 = bf16[16,1024]{1,0:T(8,128)(2,1)S(1)} custom-call(bf16[256,512]{1,0:T(8,128)(2,1)} %x_hbm.1, bf16[16,1280]{1,0:T(8,128)(2,1)} %bitcast.15, bf16[16,2,1024,128]{3,2,1,0:T(8,128)(2,1)} %bitcast.10, s32[16]{0:T(128)} %lens_hbm.1, bf16[1024,512]{1,0:T(8,128)(2,1)} %wo_hbm.1, f32[1,512]{1,0:T(1,128)} %bitcast.16, bf16[512,1024]{1,0:T(8,128)(2,1)} %bitcast.13, ...), custom_call_target="tpu_custom_call" | custom-call | flops 1000000000 | bytes 19000000 | tf_op jit(solution)/shard_map/frame/pallas_call | solution.py:501
  42.2 0.6 %copy.14 = bf16[16,1,1024]{2,0,1:T(8,128)(2,1)} copy(bf16[16,1,1024]{2,0,1:T(8,128)(2,1)S(1)} %bitcast.9) | data formatting | bytes 65536

commit v8 on v7

--- a/solution.py
+++ b/solution.py
@@ -96,7 +96,7 @@
     sibling = (chip * 2 + other, t)
 
     def step_of(d):
-        return ((0, 0), (0, 1), (0, 3), (1, 0), (0, 2), (1, 1), (1, 3), (1, 2))[d]
+        return ((0, 0), (0, 1), (0, 3), (0, 2), (1, 0), (1, 1), (1, 3), (1, 2))[d]
 
     def at(i, d):
         hi, lo = step_of(d)

time: 42.9 us -> 43 us (level)
  no operation moved by 1% of the time
where the time goes in v8:
time: 43 us; the launch traced here: 42.8 us
  Pallas kernels  42.2 us (98%)
  local copies, waits for them, and re-layouts  0.62 us (1%)
    pallas_call x1, Pallas kernels, shards(): pl.pallas_call(frame_kernel, name='frame', out_shape=jax.ShapeDtypeStruct...  42.2 us

profile of v8, /device:TPU:0, one launch (start us, length us, event | category | flops | bytes accessed | tf_op | source)
XLA Modules:
  0.0 42.8 jit_solution(2370389573768168441)
XLA Ops:
  0.0 42.2 %frame.1 = bf16[16,1024]{1,0:T(8,128)(2,1)S(1)} custom-call(bf16[256,512]{1,0:T(8,128)(2,1)} %x_hbm.1, bf16[16,1280]{1,0:T(8,128)(2,1)} %bitcast.15, bf16[16,2,1024,128]{3,2,1,0:T(8,128)(2,1)} %bitcast.10, s32[16]{0:T(128)} %lens_hbm.1, bf16[1024,512]{1,0:T(8,128)(2,1)} %wo_hbm.1, f32[1,512]{1,0:T(1,128)} %bitcast.16, bf16[512,1024]{1,0:T(8,128)(2,1)} %bitcast.13, ...), custom_call_target="tpu_custom_call" | custom-call | flops 1000000000 | bytes 19000000 | tf_op jit(solution)/shard_map/frame/pallas_call | solution.py:501
  42.2 0.6 %copy.14 = bf16[16,1,1024]{2,0,1:T(8,128)(2,1)} copy(bf16[16,1,1024]{2,0,1:T(8,128)(2,1)S(1)} %bitcast.9) | data formatting | bytes 65536
